TPU v7x, 32 devices: a whole 2x2x4 slice. The times are simulated.
32 devices in a mesh: group: 2 (over y), gx: 4 (over z), gy: 4 (over x, core).
Axes of the slice: x: 2, y: 2, z: 4, core: 2. Of those that a mesh axis runs over, the one named last changes fastest.
Arguments:
- positions: float32 [3, 8, 4, 256], P(None, ('group', 'gx'), 'gy'), parts along dimension 1
- species: int32 [8, 4, 256], P(('group', 'gx'), 'gy'), parts along dimension 0, may hold values from 0 to 7
- neighbours: int32 [8, 4, 64, 256], P(('group', 'gx'), 'gy'), parts along dimension 0, may hold values from 0 to 1279, as said below
- counts: int32 [8, 4, 256], P(('group', 'gx'), 'gy'), parts along dimension 0, may hold values from 8 to 64, as said below
- ghost_list: int32 [8, 4, 8, 128], P(('group', 'gx'), 'gy'), parts along dimension 0, may hold values from 0 to 255, as said below
- wave_index: int32 [3, 2048], replicated, may hold values from -4 to 26, as said below
- embedding: float32 [8, 64], replicated, may hold values from -6 to 6
- radial_weight: float32 [8, 64], replicated, may hold values from -2 to 2
- product_weight: float32 [128, 64], replicated, may hold values from -0.5 to 0.5
- readout_weight: float32 [64], replicated, may hold values from -0.75 to 0.75
- charge_weight: float32 [64, 64], replicated, may hold values from -0.75 to 0.75
Outputs:
- forces: float32 [3, 8, 4, 256], P(None, ('group', 'gx'), 'gy'), parts along dimension 1
- site_energy: float32 [8, 4, 256], P(('group', 'gx'), 'gy'), parts along dimension 0
There are 2 independent parts, one for each index of `group`. A program takes and returns all parts, laid end to end along the dimension named above; an argument that names none is the same for every part. Nothing has to cross between parts.
Inputs may be any that keep to these rules, and one draw needn't show every extreme that they name: `neighbours`: an entry below 256 is an own atom of the domain, else ghost column entry - 256 of step one; never the atom itself. `counts`: slots at or beyond an atom's count are padding. `ghost_list`: atoms of the sending domain. `wave_index`: the 2048 k-vectors are distinct; first row from -4 to 4, second from -4 to 4, third from 1 to 26.
All inputs are finite; a program needn't handle non-finite values.
Results may differ from a plain program's by a relative error of at most 0.0003.
Values sent between devices are 32-bit elements; how exact they have to be, the bound alone decides.
A program may use at most 64 MiB of HBM per device.

v0:
```python
import math

import jax
import jax.numpy as jnp
from jax import lax
from jax.sharding import PartitionSpec as P

DIRECTIONS = ((-1, -1), (-1, 0), (-1, 1), (0, -1), (0, 1), (1, -1), (1, 0), (1, 1))
SOFTENING = 0.01
BASIS_WIDTH = 2.0
BASIS_STEP = 0.35
SCREENING = 0.02
SLAB_HEIGHT = 2.0
PRECISE = lax.Precision.HIGHEST


def from_behind(value, axis, steps):
    count = lax.axis_size(axis)
    pairs = [(source, (source + steps) % count) for source in range(count)]
    return lax.ppermute(value, axis, pairs)


def short_range(
    ext_pos,
    ext_kind,
    neighbour_codes,
    slot_counts,
    embedding,
    radial_weight,
    product_weight,
    readout_weight,
    charge_weight,
):
    atom_count = neighbour_codes.shape[1]
    slot_count = neighbour_codes.shape[0]
    channels = embedding.shape[1]
    centre = ext_pos[:, :atom_count]
    nearby = jnp.take(ext_pos, neighbour_codes, axis=1)
    near_kind = jnp.take(ext_kind, neighbour_codes, axis=0)
    separation = nearby - centre[:, None, :]
    radius = jnp.sqrt(jnp.sum(separation * separation, axis=0) + SOFTENING)
    unit_vector = separation / radius[None]
    slot_index = lax.broadcasted_iota(jnp.int32, neighbour_codes.shape, 0)
    live_mask = (slot_index < slot_counts[None, :]).astype(ext_pos.dtype)
    centres = BASIS_STEP * jnp.arange(radial_weight.shape[0]).astype(ext_pos.dtype)
    radial = (
        jnp.exp(-BASIS_WIDTH * jnp.square(radius[None] - centres[:, None, None])) * live_mask[None]
    )
    species_ids = jnp.arange(embedding.shape[0]).astype(ext_pos.dtype)
    near_onehot = (near_kind[None] == species_ids[:, None, None]).astype(ext_pos.dtype)
    own_onehot = (ext_kind[:atom_count][None] == species_ids[:, None]).astype(ext_pos.dtype)
    density = jnp.einsum("bna,sna->bsa", radial, near_onehot, precision=PRECISE)
    oriented = unit_vector[:, None] * radial[None]
    polar_sum = jnp.einsum("xbna,sna->xbsa", oriented, near_onehot, precision=PRECISE)
    mixing = (radial_weight[:, None, :] * embedding[None, :, :]).reshape(-1, channels)
    norm_factor = 1.0 / math.sqrt(slot_count)
    scalar = norm_factor * jnp.dot(mixing.T, density.reshape(-1, atom_count), precision=PRECISE)
    scalar = scalar + jnp.dot(embedding.T, own_onehot, precision=PRECISE)
    vectorial = norm_factor * jnp.einsum(
        "kc,xka->xca", mixing, polar_sum.reshape(3, -1, atom_count), precision=PRECISE
    )
    invariants = jnp.concatenate([scalar, jnp.sum(vectorial * vectorial, axis=0)], axis=0)
    hidden = jax.nn.silu(jnp.dot(product_weight.T, invariants, precision=PRECISE))
    short_energy = jnp.dot(readout_weight, hidden, precision=PRECISE)
    charges = jnp.dot(charge_weight.T, scalar, precision=PRECISE)
    return (short_energy, charges)


def wave_table(wave_index, span_x, span_y):
    lengths = jnp.array([span_x, span_y, SLAB_HEIGHT], jnp.float32)
    return 2.0 * math.pi * wave_index.astype(jnp.float32) / lengths[:, None]


def wave_weight(wave_vectors):
    squared = jnp.sum(wave_vectors * wave_vectors, axis=0)
    return jnp.exp(-0.5 * SCREENING * SCREENING * squared) / (squared + 1.0)


def on_device(
    positions,
    species,
    neighbours,
    counts,
    ghost_list,
    wave_index,
    embedding,
    radial_weight,
    product_weight,
    readout_weight,
    charge_weight,
):
    coords = positions[:, 0, 0, :]
    atom_kind = species[0, 0].astype(jnp.float32)
    neighbour_codes = neighbours[0, 0]
    used_slots = counts[0, 0]
    ghost_rows = ghost_list[0, 0]
    atom_count = coords.shape[1]
    ghost_width = ghost_rows.shape[1]
    record = jnp.concatenate([coords, atom_kind[None]], axis=0)
    outgoing = []
    for direction_id, (shift_x, shift_y) in enumerate(DIRECTIONS):
        ghost_piece = jnp.take(record, ghost_rows[direction_id], axis=1)
        offset = jnp.array([shift_x, shift_y, 0.0, 0.0], jnp.float32)
        outgoing.append(ghost_piece - offset[:, None])
    outgoing = jnp.stack(outgoing)
    from_x = {}
    for offset_x in (1, -1):
        chosen = outgoing[5:8] if offset_x == 1 else outgoing[0:3]
        from_x[offset_x] = from_behind(chosen, "gx", offset_x)
    from_y = {}
    for offset_y in (1, -1):
        column = 2 if offset_y == 1 else 0
        own_id = 4 if offset_y == 1 else 3
        chosen = jnp.stack([from_x[-1][column], outgoing[own_id], from_x[1][column]])
        from_y[offset_y] = from_behind(chosen, "gy", offset_y)
    ghosts = jnp.stack(
        [
            from_y[-1][0],
            from_x[-1][1],
            from_y[1][0],
            from_y[-1][1],
            from_y[1][1],
            from_y[-1][2],
            from_x[1][1],
            from_y[1][2],
        ]
    )
    ghosts = jnp.transpose(ghosts, (1, 0, 2)).reshape(4, 8 * ghost_width)
    extended = jnp.concatenate([record, ghosts], axis=1)
    ext_kind = extended[3]

    def local_terms(points):
        return short_range(
            points,
            ext_kind,
            neighbour_codes,
            used_slots,
            embedding,
            radial_weight,
            product_weight,
            readout_weight,
            charge_weight,
        )

    (short_energy, charges), pullback = jax.vjp(local_terms, extended[:3])
    total_atoms = atom_count * lax.axis_size("gx") * lax.axis_size("gy")
    anchor = jnp.stack(
        [
            lax.axis_index("gx").astype(jnp.float32),
            lax.axis_index("gy").astype(jnp.float32),
            jnp.zeros((), jnp.float32),
        ]
    )
    placed = coords + anchor[:, None]
    wave_vectors = wave_table(wave_index, lax.axis_size("gx"), lax.axis_size("gy"))
    weights = wave_weight(wave_vectors)
    wave_count = wave_vectors.shape[1]
    block_size = min(256, wave_count)
    block_count = wave_count // block_size
    wave_blocks = jnp.transpose(wave_vectors.reshape(3, block_count, block_size), (1, 0, 2))
    channels = charges.shape[0]
    charge_total = lax.psum(jnp.sum(charges, axis=1), ("gx", "gy"))
    mean_charge = charge_total / total_atoms
    neutral = charges - mean_charge[:, None]

    def one_block(wave_block):
        phases = jnp.dot(wave_block.T, placed, precision=PRECISE)
        cosine = jnp.cos(phases)
        sine_part = jnp.sin(phases)
        contract = (((1,), (1,)), ((), ()))
        block_re = lax.dot_general(cosine, neutral, contract, precision=PRECISE)
        block_im = lax.dot_general(sine_part, neutral, contract, precision=PRECISE)
        return (block_re, block_im, jnp.sum(cosine, axis=1), jnp.sum(sine_part, axis=1))

    block_re, block_im, sums_re, sums_im = lax.map(one_block, wave_blocks)
    struct_re, struct_im = lax.psum(
        (block_re.reshape(wave_count, channels), block_im.reshape(wave_count, channels)),
        ("gx", "gy"),
    )
    ewald_scale = 1.0 / math.sqrt(total_atoms)
    part_re = ((ewald_scale * weights)[:, None] * struct_re).reshape(
        block_count, block_size, channels
    )
    part_im = ((ewald_scale * weights)[:, None] * struct_im).reshape(
        block_count, block_size, channels
    )

    def accumulate(running, inputs):
        potential, pulled = running
        wave_block, block_re, block_im = inputs
        phases = jnp.dot(wave_block.T, placed, precision=PRECISE)
        cosine = jnp.cos(phases)
        sine_part = jnp.sin(phases)
        contract = (((0,), (0,)), ((), ()))
        potential = (
            potential
            + lax.dot_general(block_re, cosine, contract, precision=PRECISE)
            + lax.dot_general(block_im, sine_part, contract, precision=PRECISE)
        )
        proj_re = jnp.dot(block_re, neutral, precision=PRECISE)
        proj_im = jnp.dot(block_im, neutral, precision=PRECISE)
        pulled = pulled + jnp.dot(
            wave_block, cosine * proj_im - sine_part * proj_re, precision=PRECISE
        )
        return ((potential, pulled), None)

    start_state = (
        jnp.zeros((channels, atom_count), jnp.float32),
        jnp.zeros((3, atom_count), jnp.float32),
    )
    (potential, long_grad), ignored = lax.scan(
        accumulate, start_state, (wave_blocks, part_re, part_im)
    )
    ext_grad = pullback((jnp.ones_like(short_energy), potential))[0]
    energy = short_energy + 0.5 * jnp.sum(neutral * potential, axis=0)
    ghost_grad = jnp.transpose(ext_grad[:, atom_count:].reshape(3, 8, ghost_width), (1, 0, 2))
    back_y = {}
    for offset_y in (1, -1):
        picks = (2, 4, 7) if offset_y == 1 else (0, 3, 5)
        chosen = jnp.stack([ghost_grad[picks[0]], ghost_grad[picks[1]], ghost_grad[picks[2]]])
        back_y[offset_y] = from_behind(chosen, "gy", -offset_y)
    back_x = {}
    for offset_x in (1, -1):
        column = 2 if offset_x == 1 else 0
        own_id = 6 if offset_x == 1 else 1
        chosen = jnp.stack([back_y[-1][column], ghost_grad[own_id], back_y[1][column]])
        back_x[offset_x] = from_behind(chosen, "gx", -offset_x)
    arrived = jnp.stack(
        [
            back_x[-1][0],
            back_x[-1][1],
            back_x[-1][2],
            back_y[-1][1],
            back_y[1][1],
            back_x[1][0],
            back_x[1][1],
            back_x[1][2],
        ]
    )
    flat_values = jnp.transpose(arrived, (1, 0, 2)).reshape(3, -1)
    flat_rows = ghost_rows.reshape(-1)
    returned = jnp.zeros((3, atom_count), jnp.float32).at[:, flat_rows].add(flat_values)
    forces = -(ext_grad[:, :atom_count] + returned + long_grad)
    return (forces[:, None, None, :], energy[None, None, :])


def solution(mesh):
    in_specs = (
        P(None, ("group", "gx"), "gy", None),
        P(("group", "gx"), "gy", None),
        P(("group", "gx"), "gy", None, None),
        P(("group", "gx"), "gy", None),
        P(("group", "gx"), "gy", None, None),
        P(),
        P(),
        P(),
        P(),
        P(),
        P(),
    )
    out_specs = (P(None, ("group", "gx"), "gy", None), P(("group", "gx"), "gy", None))
    return jax.shard_map(
        on_device, mesh=mesh, in_specs=in_specs, out_specs=out_specs, check_vma=False
    )
```

profile of v0, /device:TPU:0, one launch (start us, length us, event | category | flops | bytes accessed | tf_op | source)
XLA Modules:
  0.0 571.1 jit_solution(11342277105409126299)
XLA Ops:
  14.7 3.1 collective-permute-start.1
  34.1 54.4 %gather_fusion.1 = f32[16384,3]{1,0:T(8,128)} fusion(f32[3,1280]{0,1:T(8,128)S(1)} %copy.240, s32[16384]{0:T(1024)S(1)} %broadcast_clamp_fusion), kind=kCustom, calls=%fused_computation.9 | custom fusion | bytes 458752 | tf_op jit(solution)/shard_map/jvp(jit(_take))/gather | solution.py:38
  88.5 6.6 %copy.241 = f32[64,256,3]{0,2,1:T(4,128)S(1)} copy(f32[64,256,3]{2,1,0:T(8,128)} %bitcast.317) | data formatting | bytes 393216 | tf_op jit(solution)/shard_map/jvp(jit(_take))/gather | solution.py:38
  95.1 90.5 %gather_fusion = f32[16384]{0:T(1024)S(1)} fusion(f32[1280]{0:T(1024)S(1)} %maximum_reduce_fusion, s32[16384]{0:T(1024)S(1)} %broadcast_clamp_fusion), kind=kCustom, calls=%fused_computation.8 | custom fusion | bytes 196608 | tf_op jit(solution)/shard_map/jvp(jit(_take))/gather | solution.py:39
  188.2 2.3 fusion.41
  194.4 32.6 %psum.21 = f32[64]{0:T(128)S(1)} all-reduce(f32[64]{0:T(128)S(1)} %get-tuple-element.285), channel_id=1, replica_groups=mesh['group'=2,'gx'=4,'gy'=4] {'gx','gy'}, use_global_device_ids=true, to_apply=%region_6.8 | all-reduce | flops 64 | bytes 512 | tf_op jit(solution)/shard_map/psum | solution.py:162
  227.6 50.7 %while.25 = (s32[]{:T(128)}, f32[8,256,64]{1,0,2:T(8,128)S(1)}, f32[8,256,64]{1,0,2:T(8,128)}, f32[8,3,256]{2,1,0:T(4,128)S(1)}, f32[3,256]{1,0:T(4,128)S(1)}, /*index=5*/f32[64,256]{1,0:T(8,128)S(1)}, s32[]{:T(128)}, s32[]{:T(128)}) while((s32[]{:T(128)}, f32[8,256,64]{1,0,2:T(8,128)S(1)}, f32[8,256,64]{1,0,2:T(8,128)}, ...), condition=%wide.region_8.10_spmd, body=%wide.region_7.9_spmd.sunk | while | flops 103022592 | bytes 1581153 | solution.py:175
  229.3 2.4 dynamic_update_slice.10
  235.6 2.4 dynamic_update_slice.10
  241.9 2.4 dynamic_update_slice.10
  248.3 2.4 dynamic_update_slice.10
  254.6 2.4 dynamic_update_slice.10
  260.9 2.4 dynamic_update_slice.10
  267.2 2.4 dynamic_update_slice.10
  273.5 2.4 dynamic_update_slice.10
  281.2 16.4 %fusion.32 = f32[3,8,8,256]{1,2,0,3:T(8,128)} fusion(f32[8,64,256]{1,0,2:T(8,128)S(1)} %fusion.72, f32[3,64,256]{1,0,2:T(4,128)S(1)} %broadcast_divide_fusion, f32[64,256]{0,1:T(8,128)S(1)} %copy.238, f32[8]{0:T(128)S(1)} %copy-done.25), kind=kOutput, calls=%fused_computation.53 | convolution fusion | flops 38273024 | bytes 983072 | tf_op jit(solution)/shard_map/jvp(xbna,sna->xbsa)/dot_general | solution.py:54
  297.7 2.3 copy.246
  302.0 2.3 copy.248
  304.4 6.4 %fusion.27 = (f32[8,64,256]{1,0,2:T(8,128)}, f32[3,64,256]{1,0,2:T(4,128)S(1)}) fusion(f32[3,64,256]{1,0,2:T(4,128)S(1)} %broadcast_divide_fusion, f32[8,64,256]{1,0,2:T(8,128)S(1)} %fusion.72, f32[64,256]{0,1:T(8,128)S(1)} %copy.238, f32[8]{0:T(128)S(1)} %copy-done.26, f32[3,8,8,256]{2,1,0,3:T(8,128)} %copy.248), kind=kOutput, calls=%fused_computation.48 | convolution fusion | flops 39272448 | bytes 1703968 | tf_op jit(solution)/shard_map/transpose(jvp(xbna,sna->xbsa))/dot_general | solution.py:54
  313.0 82.0 %all-reduce.4.cloned.1.call-done = (f32[2048,64]{0,1:T(8,128)}, f32[2048,64]{0,1:T(8,128)}) async-done(((f32[2048,64]{0,1:T(8,128)}, f32[2048,64]{0,1:T(8,128)}), (f32[2048,64]{0,1:T(8,128)}, f32[2048,64]{0,1:T(8,128)})) %all-reduce.4.cloned.1.call-update) | async-done | bytes 1048592 | tf_op jit(solution)/shard_map/psum | solution.py:176
  397.0 47.9 %while.26 = (s32[]{:T(128)}, f32[64,256]{1,0:T(8,128)}, f32[3,256]{1,0:T(4,128)S(1)}, f32[8,256,64]{2,1,0:T(8,128)S(1)}, f32[8,3,256]{2,1,0:T(4,128)}, /*index=5...) while((s32[]{:T(128)}, f32[64,256]{1,0:T(8,128)}, ...), condition=%wide.region_12.14_spmd.clone, body=%wide.region_11.13_spmd.clone.sunk | while | flops 206292480 | bytes 3557504 | solution.py:211
  397.0 2.2 fusion.197
  402.3 2.2 fusion.197
  408.4 2.2 fusion.197
  414.5 2.2 fusion.197
  426.6 2.2 fusion.197
  432.7 2.2 fusion.197
  438.8 2.2 fusion.197
  447.7 2.9 fusion.62
  451.7 7.7 %copy.274 = f32[64,256,3]{2,1,0:T(8,128)} copy(f32[64,256,3]{0,2,1:T(4,128)S(1)} %bitcast.322) | data formatting | bytes 393216 | tf_op jit(solution)/shard_map/transpose(jvp())/add_any | solution.py:41
  459.5 88.2 %scatter_fusion = f32[3,1280]{0,1:T(8,128)S(1)} fusion(f32[3,1280]{0,1:T(8,128)S(1)} %pad.3.clone, s32[16384]{0:T(1024)S(1)} %bitcast.325, f32[16384,3]{1,0:T(8,128)} %bitcast.316), kind=kCustom, calls=%fused_computation.10 | custom fusion | flops 49152 | bytes 655360 | tf_op jit(solution)/shard_map/transpose(jvp(jit(_take)))/scatter-add | solution.py:38
  557.0 6.1 %scatter_fusion.1 = f32[3,256]{0,1:T(8,128)S(1)} fusion(f32[3,256]{0,1:T(8,128)S(1)} %slice_add_fusion, s32[1024]{0:T(1024)S(1)} %bitcast.339, f32[1024,3]{1,0:T(8,128)S(1)} %bitcast.326), kind=kCustom, calls=%fused_computation.11 | custom fusion | flops 3072 | bytes 40960 | tf_op jit(solution)/shard_map/scatter-add | solution.py:242
  (290 shorter events, 116.0 us)
Async XLA Ops:
  7.2 293.2 %copy-start = (f32[128,64]{0,1:T(8,128)S(1)}, f32[128,64]{0,1:T(8,128)}, u32[]{:S(2)}) copy-start(f32[128,64]{0,1:T(8,128)} %param.34) | copy-start | bytes 98308
  7.2 387.8 %all-reduce.4.cloned.1.call-start = ((), (), s32[]{:S(2)}) async-start(), calls=%async_computation | async-start | bytes 2097152 | tf_op jit(solution)/shard_map/psum | solution.py:176
  14.7 15.8 %collective-permute-start.1 = (f32[3,4,128]{2,1,0:T(4,128)S(1)}, f32[3,4,128]{2,1,0:T(4,128)S(1)}, u32[]{:S(2)}, u32[]{:S(2)}) collective-permute-start(f32[3,4,128]{2,1,0:T(4,128)S(1)} %pad_maximum_fusion.3), channel_id=1, source_target_pairs={{0,4},{4,8},{8,12},{12,0},{1,5},{5,9},{9,13},{13,1},{2,6},{6,10},{... | collective-permute-start | bytes 18440 | tf_op jit(solution)/shard_map/ppermute | solution.py:20
  20.1 10.5 %collective-permute-start = (f32[3,4,128]{2,1,0:T(4,128)S(1)}, f32[3,4,128]{2,1,0:T(4,128)S(1)}, u32[]{:S(2)}, u32[]{:S(2)}) collective-permute-start(f32[3,4,128]{2,1,0:T(4,128)S(1)} %pad_maximum_fusion.2), channel_id=1, source_target_pairs={{0,12},{4,0},{8,4},{12,8},{1,13},{5,1},{9,5},{13,9},{2,14},{6,2},{... | collective-permute-start | bytes 18440 | tf_op jit(solution)/shard_map/ppermute | solution.py:20
  22.2 165.9 %copy-start.24 = (f32[8]{0:T(128)}, f32[8]{0:T(128)S(1)}, u32[]{:S(2)}) copy-start(f32[8]{0:T(128)S(1)} %iota_convert_fusion) | copy-start | bytes 100
  25.8 162.3 %copy-start.13 = (f32[64,256]{0,1:T(8,128)}, f32[64,256]{0,1:T(8,128)S(1)}, u32[]{:S(2)}) copy-start(f32[64,256]{0,1:T(8,128)S(1)} %fusion.86) | copy-start | bytes 196612
  30.2 157.9 %copy-start.29 = (f32[8]{0:T(128)}, f32[8]{0:T(128)S(1)}, u32[]{:S(2)}) copy-start(f32[8]{0:T(128)S(1)} %broadcast_multiply_fusion.3) | copy-start | bytes 100
  30.4 280.6 %copy-start.3 = (f32[3,256]{0,1:T(8,128)}, f32[3,256]{0,1:T(8,128)S(1)}, u32[]{:S(2)}) copy-start(f32[3,256]{0,1:T(8,128)S(1)} %copy.242) | copy-start | bytes 9220
  30.6 3.1 collective-permute-start.3
  30.7 3.1 collective-permute-start.2
  95.1 90.6 %copy-start.17 = (s32[1,1,64,256]{3,2,1,0:T(8,128)S(1)}, s32[1,1,64,256]{3,2,1,0:T(8,128)}, u32[]{:S(2)}) copy-start(s32[1,1,64,256]{3,2,1,0:T(8,128)} %param.28) | copy-start | bytes 196612
  186.4 5.6 copy-start.20
  187.3 39.8 %copy-start.5 = (f32[64,256]{0,1:T(8,128)}, f32[64,256]{0,1:T(8,128)S(1)}, u32[]{:S(2)}) copy-start(f32[64,256]{0,1:T(8,128)S(1)} %copy.244) | copy-start | bytes 196612
  187.3 40.3 %copy-start.14 = (f32[8,256,64]{1,0,2:T(8,128)S(1)}, f32[8,256,64]{1,0,2:T(8,128)}, u32[]{:S(2)}) copy-start(f32[8,256,64]{1,0,2:T(8,128)} %custom-call.22) | copy-start | bytes 1572868
  187.4 116.9 %copy-start.7 = (f32[64,256]{0,1:T(8,128)}, f32[64,256]{0,1:T(8,128)S(1)}, u32[]{:S(2)}) copy-start(f32[64,256]{0,1:T(8,128)S(1)} %copy.238) | copy-start | bytes 196612
  194.4 33.2 %copy-start.10 = (f32[256,64]{0,1:T(8,128)}, f32[256,64]{0,1:T(8,128)S(1)}, u32[]{:S(2)}) copy-start(f32[256,64]{0,1:T(8,128)S(1)} %get-tuple-element.286) | copy-start | bytes 196612
  227.6 53.7 %copy-start.25 = (f32[8]{0:T(128)S(1)}, f32[8]{0:T(128)}, u32[]{:S(2)}) copy-start(f32[8]{0:T(128)} %copy-done.24) | copy-start | bytes 100
  304.4 6.5 %copy-start.16 = (f32[64,256]{1,0:T(8,128)S(1)}, f32[64,256]{1,0:T(8,128)}, u32[]{:S(2)}) copy-start(f32[64,256]{1,0:T(8,128)} %get-tuple-element.239) | copy-start | bytes 196612
  304.4 90.6 %copy-start.22 = (f32[2048]{0:T(1024)S(1)}, f32[2048]{0:T(1024)}, u32[]{:S(2)}) copy-start(f32[2048]{0:T(1024)} %divide_multiply_fusion) | copy-start | bytes 24580
  310.8 85.8 %copy-start.1 = (f32[3,64,256]{1,0,2:T(4,128)}, f32[3,64,256]{1,0,2:T(4,128)S(1)}, u32[]{:S(2)}) copy-start(f32[3,64,256]{1,0,2:T(4,128)S(1)} %get-tuple-element.183) | copy-start | bytes 589828
  444.9 5.8 %copy-start.9 = (f32[64,256]{1,0:T(8,128)S(1)}, f32[64,256]{1,0:T(8,128)}, u32[]{:S(2)}) copy-start(f32[64,256]{1,0:T(8,128)} %copy-done.8) | copy-start | bytes 196612
  444.9 5.8 %copy-start.18 = (f32[64,256]{1,0:T(8,128)S(1)}, f32[64,256]{1,0:T(8,128)}, u32[]{:S(2)}) copy-start(f32[64,256]{1,0:T(8,128)} %copy.255) | copy-start | bytes 196612
  444.9 5.9 %copy-start.2 = (f32[3,64,256]{1,0,2:T(4,128)S(1)}, f32[3,64,256]{1,0,2:T(4,128)}, u32[]{:S(2)}) copy-start(f32[3,64,256]{1,0,2:T(4,128)} %copy-done.1) | copy-start | bytes 589828
  444.9 5.9 %copy-start.4 = (f32[3,256]{0,1:T(8,128)S(1)}, f32[3,256]{0,1:T(8,128)}, u32[]{:S(2)}) copy-start(f32[3,256]{0,1:T(8,128)} %copy-done.3) | copy-start | bytes 9220
  444.9 6.0 %copy-start.6 = (f32[64,256]{0,1:T(8,128)S(1)}, f32[64,256]{0,1:T(8,128)}, u32[]{:S(2)}) copy-start(f32[64,256]{0,1:T(8,128)} %copy-done.5) | copy-start | bytes 196612
  451.7 7.8 %copy-start.12 = (s32[8,2,8,128]{3,1,2,0:T(2,128)S(1)}, s32[8,2,8,128]{3,1,2,0:T(2,128)}, u32[]{:S(2)}) copy-start(s32[8,2,8,128]{3,1,2,0:T(2,128)} %copy-done.11) | copy-start | bytes 196612
  459.4 95.7 %copy-start.28 = (f32[1,256]{1,0:T(1,128)S(1)}, f32[1,256]{1,0:T(1,128)}, u32[]{:S(2)}) copy-start(f32[1,256]{1,0:T(1,128)} %fusion.104) | copy-start | bytes 3076
  459.4 97.5 %copy-start.23 = (s32[1024,1]{0,1:T(1,128)S(1)}, s32[1024,1]{0,1:T(1,128)}, u32[]{:S(2)}) copy-start(s32[1024,1]{0,1:T(1,128)} %compare_select_fusion.2) | copy-start | bytes 12292
  547.9 3.1 collective-permute-start.4
  548.1 3.1 collective-permute-start.5
  551.3 5.4 collective-permute-start.6
  553.0 3.7 collective-permute-start.7
  (8 other events, 18.5 us)
Sparse Core Ops, SparseCore 0:
  304.5 90.4 all-reduce.3
where the time goes:
time: 581 us; the launch traced here: 571 us
  local copies, waits for them, and re-layouts  208 us (36%)
  other arithmetic  111 us (19%)
  matrix products  104 us (18%)
  waiting for transfers between devices  85.8 us (15%)
  blocking collectives  32.6 us (6%)
  between operations  15.4 us (3%)
  starting transfers between devices  12.7 us (2%)
    gather x2, local copies, waits for them, and re-layouts, short_range(): near_kind = jnp.take(ext_kind, neighbour_codes, axis=0)  90.6 us
    scatter-add x1, other arithmetic, short_range(): nearby = jnp.take(ext_pos, neighbour_codes, axis=1)  88.2 us
    psum x1, waiting for transfers between devices, on_device(): lax.psum((block_re.reshape(wave_count, channels), block_im.reshape(wave_c...  82 us
    gather x2, local copies, waits for them, and re-layouts, short_range(): nearby = jnp.take(ext_pos, neighbour_codes, axis=1)  61 us
    psum x1, blocking collectives, on_device(): charge_total = lax.psum(jnp.sum(charges, axis=1), ('gx', 'gy'))  32.6 us
    dynamic_update_slice x32, local copies, waits for them, and re-layouts, on_device(): block_re, block_im, sums_re, sums_im = lax.map(one_block, wave_blocks)  27.4 us
    dot_general x2, matrix products, short_range(): jnp.einsum('xbna,sna->xbsa', oriented, near_onehot, precision=PRECISE)  22.9 us
    dot_general x8, matrix products, accumulate(): phases = jnp.dot(wave_block.T, placed, precision=PRECISE)  17.8 us
  transfers between devices with their start and end apart: 9, of which 5 were waited for; matrix products, arithmetic and copies ran while one was open for 3% of the time, Pallas kernels for 0%

commit v1 on v0

v1 whole, which is shorter than its diff:
```python
import functools
import math

import jax
import jax.numpy as jnp
import numpy as np
from jax import lax
from jax.experimental import pallas as pl
from jax.experimental.pallas import tpu as pltpu
from jax.sharding import PartitionSpec as P

DIRECTIONS = ((-1, -1), (-1, 0), (-1, 1), (0, -1), (0, 1), (1, -1), (1, 0), (1, 1))
SOFTENING = 0.01
BASIS_WIDTH = 2.0
BASIS_STEP = 0.35
SCREENING = 0.02
SLAB_HEIGHT = 2.0
PRECISE = lax.Precision.HIGHEST
MESH = pl.DeviceIdType.MESH
LANES = 128
SUBLANES = 8
VMEM_LIMIT = 40 * 1024 * 1024
F32 = jnp.float32
BF16 = jnp.bfloat16
VMEM = pltpu.VMEM


def half_turn_series(odd, terms):
    nodes = 0.125 * (1.0 + np.cos(np.pi * (np.arange(64) + 0.5) / 64))
    root = np.sqrt(nodes)
    values = np.sin(np.pi * root) / root if odd else np.cos(np.pi * root)
    series = np.polynomial.chebyshev.Chebyshev.fit(nodes, values, terms - 1, domain=[0.0, 0.25])
    return [float(c) for c in series.convert(kind=np.polynomial.Polynomial).coef]


SIN_SERIES = half_turn_series(True, 6)
COS_SERIES = half_turn_series(False, 6)


def horner(series, square):
    total = jnp.full_like(square, series[-1])
    for coefficient in reversed(series[:-1]):
        total = total * square + coefficient
    return total


def cos_sin_turns(turns):
    reduced = turns - jnp.round(turns)
    square = reduced * reduced
    half_sin = reduced * horner(SIN_SERIES, square)
    half_cos = horner(COS_SERIES, square)
    return 1.0 - 2.0 * (half_sin * half_sin), 2.0 * (half_sin * half_cos)


def dot_nn(a, b):
    return lax.dot_general(
        a, b, (((1,), (0,)), ((), ())), precision=PRECISE, preferred_element_type=F32
    )


def dot_tn(a, b):
    return lax.dot_general(
        a, b, (((0,), (0,)), ((), ())), precision=PRECISE, preferred_element_type=F32
    )


def split_bf16(value):
    high = value.astype(BF16)
    return high, (value - high.astype(F32)).astype(BF16)


def dot3(a, b, dims):
    a_high, a_low = split_bf16(a)
    b_high, b_low = split_bf16(b)
    dot = functools.partial(
        lax.dot_general, dimension_numbers=(dims, ((), ())), preferred_element_type=F32
    )
    return dot(a_high, b_high) + (dot(a_high, b_low) + dot(a_low, b_high))


def lookup(table_row, codes):
    rows = codes.shape[0]
    pieces = []
    for part in range(codes.shape[1] // LANES):
        code = codes[:, part * LANES : (part + 1) * LANES]
        low, high = code % LANES, code // LANES
        found = jnp.zeros((rows, LANES), F32)
        for chunk in range(table_row.shape[1] // LANES):
            table = jnp.broadcast_to(
                table_row[:, chunk * LANES : (chunk + 1) * LANES], (rows, LANES)
            )
            picked = jnp.take_along_axis(table, low, axis=1)
            found = jnp.where(high == chunk, picked, found)
        pieces.append(found)
    return jnp.concatenate(pieces, axis=1)


def pick_kernel(record_ref, rows_ref, out_ref):
    rows = rows_ref[...]
    for field in range(4):
        found = lookup(record_ref[field : field + 1, :], rows)
        for direction, shift in enumerate(DIRECTIONS):
            offset = float(shift[field]) if field < 2 else 0.0
            out_ref[direction, field : field + 1, :] = found[direction : direction + 1] - offset
    for direction in range(len(DIRECTIONS)):
        out_ref[direction, 4:, :] = jnp.zeros((4, rows.shape[1]), F32)


def swap_kernel(sign, nx, ny, in_ref, out_ref, send_sem, recv_sem):
    gx, gy = lax.axis_index("gx"), lax.axis_index("gy")
    targets = [
        {
            "gx": lax.rem(gx + sign * sx + nx, nx),
            "gy": lax.rem(gy + sign * sy + ny, ny),
        }
        for sx, sy in DIRECTIONS
    ]
    barrier = pltpu.get_barrier_semaphore()
    for target in targets:
        pl.semaphore_signal(barrier, inc=1, device_id=target, device_id_type=MESH)
    pl.semaphore_wait(barrier, len(targets))
    copies = [
        pltpu.make_async_remote_copy(
            src_ref=in_ref.at[d],
            dst_ref=out_ref.at[d],
            send_sem=send_sem.at[d],
            recv_sem=recv_sem.at[d],
            device_id=target,
            device_id_type=MESH,
        )
        for d, target in enumerate(targets)
    ]
    for copy in copies:
        copy.start()
    for copy in copies:
        copy.wait()


def swap_blocks(blocks, sign, nx, ny, collective_id):
    count = blocks.shape[0]
    return pl.pallas_call(
        functools.partial(swap_kernel, sign, nx, ny),
        name="ghosts_out" if sign == 1 else "ghosts_back",
        out_shape=jax.ShapeDtypeStruct(blocks.shape, F32),
        in_specs=[pl.BlockSpec(memory_space=VMEM)],
        out_specs=pl.BlockSpec(memory_space=VMEM),
        scratch_shapes=[pltpu.SemaphoreType.DMA((count,)), pltpu.SemaphoreType.DMA((count,))],
        compiler_params=pltpu.CompilerParams(collective_id=collective_id, has_side_effects=True),
    )(blocks)


def gather_kernel(nx, ny, in_ref, out_ref, own_sem, line_sem, cross_sem, pair_sem, recv_sem):
    gx, gy = lax.axis_index("gx"), lax.axis_index("gy")
    chips = ny // 2
    core = lax.rem(gy, 2)
    chip = gy // 2
    peer = chip * 2 + (1 - core)
    order = sorted(range(1, nx), key=lambda step: min(step, nx - step))
    lines = [lax.rem(gx + step, nx) for step in order]
    crosses = [lax.rem(chip + step, chips) * 2 + core for step in range(1, chips)]
    partners = [{"gx": x} for x in lines] + [{"gy": y} for y in crosses] + [{"gy": peer}]
    barrier = pltpu.get_barrier_semaphore()
    for partner in partners:
        pl.semaphore_signal(barrier, inc=1, device_id=partner, device_id_type=MESH)
    pl.semaphore_wait(barrier, len(partners))

    def remote(source, slot_x, slot_y, send, device):
        return pltpu.make_async_remote_copy(
            src_ref=source,
            dst_ref=out_ref.at[slot_x, slot_y],
            send_sem=send,
            recv_sem=recv_sem.at[slot_x, slot_y],
            device_id=device,
            device_id_type=MESH,
        )

    def arrived(slot_x, slot_y):
        remote(
            out_ref.at[slot_x, slot_y], slot_x, slot_y, recv_sem.at[slot_x, slot_y], {"gy": peer}
        ).wait_recv()

    sent = []

    def send(source, slot_x, slot_y, semaphore, device):
        copy = remote(source, slot_x, slot_y, semaphore, device)
        copy.start()
        sent.append(copy)

    own = pltpu.make_async_copy(in_ref, out_ref.at[gx, gy], own_sem)
    for index, x in enumerate(lines):
        send(in_ref, gx, gy, line_sem.at[index], {"gx": x})
    for index, y in enumerate(crosses):
        send(in_ref, gx, gy, cross_sem.at[0, index], {"gy": y})
    send(in_ref, gx, gy, pair_sem.at[0, 0], {"gy": peer})
    own.start()
    for row, x in enumerate(lines):
        arrived(x, gy)
        for index, y in enumerate(crosses):
            send(out_ref.at[x, gy], x, gy, cross_sem.at[row + 1, index], {"gy": y})
        send(out_ref.at[x, gy], x, gy, pair_sem.at[row + 1, 0], {"gy": peer})
    for row, x in enumerate([gx] + lines):
        for index, y in enumerate(crosses):
            arrived(x, y)
            send(out_ref.at[x, y], x, y, pair_sem.at[row, index + 1], {"gy": peer})
    for x in [gx] + lines:
        for step in range(chips):
            arrived(x, lax.rem(chip + step, chips) * 2 + (1 - core))
    own.wait()
    for copy in sent:
        copy.wait_send()


def gather_blocks(block, nx, ny, collective_id, name):
    chips = ny // 2
    return pl.pallas_call(
        functools.partial(gather_kernel, nx, ny),
        name=name,
        out_shape=jax.ShapeDtypeStruct((nx, ny) + block.shape, F32),
        in_specs=[pl.BlockSpec(memory_space=VMEM)],
        out_specs=pl.BlockSpec(memory_space=VMEM),
        scratch_shapes=[
            pltpu.SemaphoreType.DMA,
            pltpu.SemaphoreType.DMA((nx - 1,)),
            pltpu.SemaphoreType.DMA((nx, max(chips - 1, 1))),
            pltpu.SemaphoreType.DMA((nx, chips)),
            pltpu.SemaphoreType.DMA((nx, ny)),
        ],
        compiler_params=pltpu.CompilerParams(
            collective_id=collective_id, has_side_effects=True, vmem_limit_bytes=VMEM_LIMIT
        ),
    )(block)


def mixing_of(radial_weight, embedding):
    return jnp.concatenate(
        [radial_weight[b : b + 1, :] * embedding for b in range(radial_weight.shape[0])], axis=0
    )


def short_kernel(
    record_ref, ghost_ref, codes_ref, counts_ref, anchor_ref,
    emb_ref, rw_ref, pw_ref, ro_ref, cw_ref,
    block_ref, energy_ref, geo_ref, gd_ref, gp_ref,
    terms_ref, moments_ref,
):
    slots, atoms = codes_ref.shape
    species, channels = emb_ref.shape
    basis = rw_ref.shape[0]
    codes = codes_ref[...]
    near = []
    for field in range(4):
        row = jnp.concatenate(
            [record_ref[field : field + 1, :]]
            + [ghost_ref[d, field : field + 1, :] for d in range(ghost_ref.shape[0])],
            axis=1,
        )
        near.append(lookup(row, codes))
    separation = [near[x] - record_ref[x : x + 1, :] for x in range(3)]
    square = separation[0] * separation[0]
    square = square + separation[1] * separation[1] + separation[2] * separation[2]
    radius = jnp.sqrt(square + SOFTENING)
    inverse = 1.0 / radius
    kind = near[3]
    slot = lax.broadcasted_iota(jnp.int32, (slots, atoms), 0)
    live = jnp.where(slot < counts_ref[...], 1.0, 0.0)
    unit = [part * inverse for part in separation]
    for x in range(3):
        geo_ref[x] = unit[x]
    geo_ref[3] = radius
    geo_ref[4] = kind
    for b in range(basis):
        offset = radius - BASIS_STEP * b
        radial = jnp.exp(-BASIS_WIDTH * (offset * offset)) * live
        terms_ref[b] = radial
        for x in range(3):
            terms_ref[(x + 1) * basis + b] = unit[x] * radial

    def reduce_term(q, carry):
        term = terms_ref[q]
        near_kind = geo_ref[4]
        rows = [
            jnp.sum(jnp.where(near_kind == float(s), term, 0.0), axis=0, keepdims=True)
            for s in range(species)
        ]
        moments_ref[q] = jnp.concatenate(rows, axis=0)
        return carry

    lax.fori_loop(0, 4 * basis, reduce_term, 0, unroll=2)
    mixing = mixing_of(rw_ref[...], emb_ref[...])
    norm = 1.0 / math.sqrt(slots)
    moments = [
        moments_ref[q * basis : (q + 1) * basis].reshape(basis * species, atoms) for q in range(4)
    ]
    own_species = lax.broadcasted_iota(jnp.int32, (species, atoms), 0).astype(F32)
    onehot = jnp.where(own_species == record_ref[3:4, :], 1.0, 0.0)
    scalar = norm * dot_tn(mixing, moments[0]) + dot_tn(emb_ref[...], onehot)
    vectorial = [norm * dot_tn(mixing, moments[x + 1]) for x in range(3)]
    squares = vectorial[0] * vectorial[0] + vectorial[1] * vectorial[1] + vectorial[2] * vectorial[2]
    invariants = jnp.concatenate([scalar, squares], axis=0)
    before = dot_tn(pw_ref[...], invariants)
    gate = 1.0 / (1.0 + jnp.exp(-before))
    hidden = before * gate
    energy_ref[...] = jnp.sum(hidden * ro_ref[...], axis=0, keepdims=True)
    block_ref[:channels, :] = dot_tn(cw_ref[...], scalar)
    block_ref[channels : channels + 3, :] = record_ref[:3, :] + anchor_ref[...]
    block_ref[channels + 3 :, :] = jnp.zeros((SUBLANES - 3, atoms), F32)
    slope = ro_ref[...] * (gate + hidden * (1.0 - gate))
    back = dot_nn(pw_ref[...], slope)
    gd_ref[...] = norm * dot_nn(mixing, back[:channels])
    for x in range(3):
        grad = norm * dot_nn(mixing, 2.0 * vectorial[x] * back[channels:])
        gp_ref[x * basis : (x + 1) * basis] = grad.reshape(basis, species, atoms)


def structure_kernel(neutralise, total, channels, spans, blocks_ref, cols_ref, rows_ref, out_ref, mean_ref):
    domains = blocks_ref.shape[0]
    wave_blocks = out_ref.shape[0]
    atoms = blocks_ref.shape[2]
    if neutralise:
        summed = blocks_ref[0, :channels, :]
        for d in range(1, domains):
            summed = summed + blocks_ref[d, :channels, :]
        mean = jnp.sum(summed, axis=1, keepdims=True) / total
    else:
        mean = jnp.zeros((channels, 1), F32)
    mean_ref[...] = jnp.broadcast_to(mean, mean_ref.shape)

    def one_block(w, carry):
        cols = cols_ref[pl.ds(pl.multiple_of(w * LANES, LANES), LANES), :]

        def add_domain(d, running):
            block = blocks_ref[d]
            turns = cols[:, 0:1] * (block[channels : channels + 1] * (1.0 / spans[0]))
            turns = turns + cols[:, 1:2] * (block[channels + 1 : channels + 2] * (1.0 / spans[1]))
            turns = turns + cols[:, 2:3] * (block[channels + 2 : channels + 3] * (1.0 / spans[2]))
            cosine, sine = cos_sin_turns(turns)
            waves = jnp.concatenate([cosine, sine], axis=0)
            return running + dot3(block[:channels] - mean, waves, ((1,), (1,)))

        summed = lax.fori_loop(0, domains, add_domain, jnp.zeros((channels, 2 * LANES), F32))
        rows = rows_ref[w]
        squared = jnp.zeros((1, LANES), F32)
        for x in range(3):
            wave = rows[x : x + 1] * (2.0 * math.pi / spans[x])
            squared = squared + wave * wave
        weight = jnp.exp(-0.5 * SCREENING * SCREENING * squared) / (squared + 1.0)
        weight = weight * (1.0 / math.sqrt(total))
        out_ref[w] = summed * jnp.concatenate([weight, weight], axis=1)
        return carry

    lax.fori_loop(0, wave_blocks, one_block, 0)


def back_kernel(
    spans, struct_ref, cols_ref, rows_ref, block_ref, mean_ref, short_ref, geo_ref, codes_ref,
    counts_ref, gd_ref, gp_ref, rw_ref, emb_ref, cw_ref,
    energy_ref, own_ref, ghost_ref,
    gd_rows_ref, pair_ref, acc_ref,
):
    slots, atoms = codes_ref.shape
    species, channels = emb_ref.shape
    basis = rw_ref.shape[0]
    wave_blocks = struct_ref.shape[0]
    neutral = block_ref[:channels, :] - mean_ref[:, 0:1]
    neutral_high, neutral_low = split_bf16(neutral)
    scaled = [block_ref[channels + x : channels + x + 1, :] * (1.0 / spans[x]) for x in range(3)]
    over_rows = ((0,), (0,))

    def add_waves(w, carry):
        potential, pulled = carry
        cols = cols_ref[pl.ds(pl.multiple_of(w * LANES, LANES), LANES), :]
        turns = cols[:, 0:1] * scaled[0] + cols[:, 1:2] * scaled[1] + cols[:, 2:3] * scaled[2]
        cosine, sine = cos_sin_turns(turns)
        waves = jnp.concatenate([cosine, sine], axis=0)
        struct = struct_ref[w]
        potential = potential + dot3(struct, waves, ((1,), (0,)))
        high, low = split_bf16(struct)
        dot = functools.partial(
            lax.dot_general, dimension_numbers=(over_rows, ((), ())), preferred_element_type=F32
        )
        projected = dot(high, neutral_high) + (dot(high, neutral_low) + dot(low, neutral_high))
        torque = cosine * projected[LANES:] - sine * projected[:LANES]
        return potential, pulled + dot3(rows_ref[w], torque, ((1,), (0,)))

    potential, pulled = lax.fori_loop(
        0,
        wave_blocks,
        add_waves,
        (jnp.zeros((channels, atoms), F32), jnp.zeros((SUBLANES, atoms), F32)),
    )
    energy_ref[...] = short_ref[...] + 0.5 * jnp.sum(neutral * potential, axis=0, keepdims=True)
    mixing = mixing_of(rw_ref[...], emb_ref[...])
    norm = 1.0 / math.sqrt(slots)
    density_grad = gd_ref[...] + norm * dot_nn(mixing, dot_nn(cw_ref[...], potential))
    gd_rows_ref[...] = density_grad.reshape(basis, species, atoms)

    def pair_rows(i, carry):
        start = pl.multiple_of(i * SUBLANES, SUBLANES)
        window = pl.ds(start, SUBLANES)
        unit = [geo_ref[x, window, :] for x in range(3)]
        radius = geo_ref[3, window, :]
        kind = geo_ref[4, window, :]
        masks = [kind == float(s) for s in range(1, species)]
        slot = lax.broadcasted_iota(jnp.int32, (SUBLANES, atoms), 0) + start
        live = jnp.where(slot < counts_ref[...], 1.0, 0.0)

        def of_kind(table):
            chosen = jnp.broadcast_to(table[0:1, :], (SUBLANES, atoms))
            for s in range(1, species):
                chosen = jnp.where(masks[s - 1], table[s : s + 1, :], chosen)
            return chosen

        along = jnp.zeros((SUBLANES, atoms), F32)
        turn = [jnp.zeros((SUBLANES, atoms), F32) for x in range(3)]
        for b in range(basis):
            offset = radius - BASIS_STEP * b
            radial = jnp.exp(-BASIS_WIDTH * (offset * offset)) * live
            total = of_kind(gd_rows_ref[b])
            for x in range(3):
                polar = of_kind(gp_ref[x * basis + b])
                total = total + unit[x] * polar
                turn[x] = turn[x] + radial * polar
            along = along + (-2.0 * BASIS_WIDTH) * offset * radial * total
        inverse = 1.0 / radius
        swing = turn[0] * unit[0] + turn[1] * unit[1] + turn[2] * unit[2]
        radial_part = along - swing * inverse
        for x in range(3):
            pair_ref[x, window, :] = unit[x] * radial_part + turn[x] * inverse
        return carry

    lax.fori_loop(0, slots // SUBLANES, pair_rows, 0)
    chunks = acc_ref.shape[0] // 6
    acc_ref[...] = jnp.zeros(acc_ref.shape, F32)
    group = 4

    def scatter_rows(i, carry):
        start = i * group
        total = None
        for k in range(group):
            code = codes_ref[pl.ds(start + k, 1), :]
            low, high = code % LANES, code // LANES
            spots = lax.broadcasted_iota(jnp.int32, (LANES, atoms), 0)
            onehot = jnp.where(spots == low, 1.0, 0.0).astype(BF16)
            chunk_ids = lax.broadcasted_iota(jnp.int32, (chunks, atoms), 0)
            here = chunk_ids == high
            values = jnp.concatenate(
                [jnp.where(here, pair_ref[x, pl.ds(start + k, 1), :], 0.0) for x in range(3)],
                axis=0,
            )
            values = jnp.concatenate(split_bf16(values), axis=0)
            part = lax.dot_general(
                values, onehot, (((1,), (1,)), ((), ())), preferred_element_type=F32
            )
            total = part if total is None else total + part
        acc_ref[...] += total
        return carry

    lax.fori_loop(0, slots // group, scatter_rows, 0)
    summed = acc_ref[: 3 * chunks, :] + acc_ref[3 * chunks :, :]
    own_chunks = atoms // LANES
    own_ref[...] = jnp.zeros(own_ref.shape, F32)
    ghost_ref[...] = jnp.zeros(ghost_ref.shape, F32)
    for x in range(3):
        received = jnp.concatenate(
            [summed[x * chunks + h : x * chunks + h + 1, :] for h in range(own_chunks)], axis=1
        )
        centre = jnp.sum(pair_ref[x], axis=0, keepdims=True)
        wave_pull = pulled[x : x + 1, :] * (2.0 * math.pi / spans[x])
        own_ref[x : x + 1, :] = received - centre + wave_pull
        for d in range(ghost_ref.shape[0]):
            row = x * chunks + own_chunks + d
            ghost_ref[d, x : x + 1, :] = summed[row : row + 1, :]


def owners_kernel(back_ref, rows_ref, own_ref, out_ref):
    atoms = own_ref.shape[1]
    total = own_ref[...]
    for d in range(back_ref.shape[0]):
        spots = lax.broadcasted_iota(jnp.int32, (atoms, rows_ref.shape[1]), 0)
        onehot = jnp.where(spots == rows_ref[d : d + 1, :], 1.0, 0.0).astype(BF16)
        values = jnp.concatenate(split_bf16(back_ref[d]), axis=0)
        part = lax.dot_general(values, onehot, (((1,), (1,)), ((), ())), preferred_element_type=F32)
        total = total + part[:SUBLANES] + part[SUBLANES:]
    out_ref[...] = -total[:3]


def local_call(kernel, name, outs, scratch, *args):
    return pl.pallas_call(
        kernel,
        name=name,
        out_shape=[jax.ShapeDtypeStruct(shape, F32) for shape in outs],
        in_specs=[pl.BlockSpec(memory_space=VMEM)] * len(args),
        out_specs=[pl.BlockSpec(memory_space=VMEM)] * len(outs),
        scratch_shapes=[pltpu.VMEM(shape, F32) for shape in scratch],
        compiler_params=pltpu.CompilerParams(vmem_limit_bytes=VMEM_LIMIT),
    )(*args)


def on_device(
    positions,
    species,
    neighbours,
    counts,
    ghost_list,
    wave_index,
    embedding,
    radial_weight,
    product_weight,
    readout_weight,
    charge_weight,
):
    nx, ny = lax.axis_size("gx"), lax.axis_size("gy")
    domains = nx * ny
    atoms = positions.shape[3]
    codes = neighbours[0, 0]
    slots = codes.shape[0]
    used = counts[0]
    ghost_rows = ghost_list[0, 0]
    directions, width = ghost_rows.shape
    waves = wave_index.shape[1]
    kinds, channels = embedding.shape
    basis = radial_weight.shape[0]
    spans = (float(nx), float(ny), SLAB_HEIGHT)
    total_atoms = float(atoms * domains)
    gx, gy = lax.axis_index("gx"), lax.axis_index("gy")
    record = jnp.concatenate(
        [positions.reshape(3, atoms), species[0].astype(F32)], axis=0
    )
    anchor = jnp.stack([gx.astype(F32), gy.astype(F32), jnp.zeros((), F32)]).reshape(3, 1)
    wave_float = wave_index.astype(F32)
    wave_cols = wave_float.T
    wave_rows = jnp.pad(
        wave_float.reshape(3, waves // LANES, LANES).transpose(1, 0, 2), ((0, 0), (0, 5), (0, 0))
    )
    readout = readout_weight.reshape(channels, 1)

    (outgoing,) = local_call(
        pick_kernel, "pick_ghosts", [(directions, SUBLANES, width)], [], record, ghost_rows
    )
    ghosts = swap_blocks(outgoing, 1, nx, ny, 0)
    block, short_energy, geometry, density_grad, polar_grad = local_call(
        short_kernel,
        "short_range",
        [
            (channels + SUBLANES, atoms),
            (1, atoms),
            (5, slots, atoms),
            (basis * kinds, atoms),
            (3 * basis, kinds, atoms),
        ],
        [(4 * basis, slots, atoms), (4 * basis, kinds, atoms)],
        record, ghosts, codes, used, anchor,
        embedding, radial_weight, product_weight, readout, charge_weight,
    )
    wave_blocks = waves // LANES
    if wave_blocks == domains:
        mine = gx * ny + gy
        blocks = gather_blocks(block, nx, ny, 1, "gather_charges")
        struct, mean = local_call(
            functools.partial(structure_kernel, True, total_atoms, channels, spans),
            "structure",
            [(1, channels, 2 * LANES), (channels, LANES)],
            [],
            blocks.reshape(domains, channels + SUBLANES, atoms),
            lax.dynamic_slice_in_dim(wave_cols, mine * LANES, LANES, axis=0),
            lax.dynamic_slice_in_dim(wave_rows, mine, 1, axis=0),
        )
        struct = gather_blocks(struct[0], nx, ny, 2, "gather_structure")
        struct = struct.reshape(wave_blocks, channels, 2 * LANES)
    else:
        charge_total = lax.psum(jnp.sum(block[:channels], axis=1, keepdims=True), ("gx", "gy"))
        mean = jnp.broadcast_to(charge_total / total_atoms, (channels, LANES))
        neutral = jnp.concatenate([block[:channels] - mean[:, :1], block[channels:]], axis=0)
        struct, unused = local_call(
            functools.partial(structure_kernel, False, total_atoms, channels, spans),
            "structure",
            [(wave_blocks, channels, 2 * LANES), (channels, LANES)],
            [],
            neutral[None],
            wave_cols,
            wave_rows,
        )
        struct = lax.psum(struct, ("gx", "gy"))
    chunks = 16 * -(-(atoms // LANES + directions * width // LANES) // 16)
    energy, own_grad, ghost_grad = local_call(
        functools.partial(back_kernel, spans),
        "gradients",
        [(1, atoms), (SUBLANES, atoms), (directions, SUBLANES, width)],
        [(basis, kinds, atoms), (3, slots, atoms), (6 * chunks, LANES)],
        struct, wave_cols, wave_rows, block, mean, short_energy, geometry, codes, used,
        density_grad, polar_grad, radial_weight, embedding, charge_weight,
    )
    back = swap_blocks(ghost_grad, -1, nx, ny, 3)
    (forces,) = local_call(owners_kernel, "owners", [(3, atoms)], [], back, ghost_rows, own_grad)
    return (forces[:, None, None, :], energy[None])


def solution(mesh):
    in_specs = (
        P(None, ("group", "gx"), "gy", None),
        P(("group", "gx"), "gy", None),
        P(("group", "gx"), "gy", None, None),
        P(("group", "gx"), "gy", None),
        P(("group", "gx"), "gy", None, None),
        P(),
        P(),
        P(),
        P(),
        P(),
        P(),
    )
    out_specs = (P(None, ("group", "gx"), "gy", None), P(("group", "gx"), "gy", None))
    return jax.shard_map(
        on_device, mesh=mesh, in_specs=in_specs, out_specs=out_specs, check_vma=False
    )
```

time: 581 us -> 83.3 us (0.14); the launches traced: 571 us -> 82.9 us
  local copies, waits for them, and re-layouts: 208 us -> 4.02 us
  other arithmetic: 111 us -> 0.88 us
  matrix products: 104 us -> 0 us
  waiting for transfers between devices: 85.8 us -> 0 us
  Pallas kernels: 0 us -> 77.1 us
  blocking collectives: 32.6 us -> 0 us
  between operations: 15.4 us -> 0.91 us
  starting transfers between devices: 12.7 us -> 0 us
    gather x12 -> x0, local copies, waits for them, and re-layouts: 157 us -> none  [the longest x2 90.6 us: short_range(): near_kind = jnp.take(ext_kind, neighbour_codes, axis=0)]
    dot_general x86 -> x0, matrix products: 104 us -> none  [the longest x2 22.9 us: short_range(): jnp.einsum('xbna,sna->xbsa', oriented, near_onehot, precision=PRECISE)]
    scatter-add x2 -> x0, other arithmetic: 94.3 us -> none  [the longest x1 88.2 us: short_range(): nearby = jnp.take(ext_pos, neighbour_codes, axis=1)]
    psum x1 -> x0, waiting for transfers between devices: 82 us -> none  [on_device(): lax.psum((block_re.reshape(wave_count, channels), block_im.reshape(wave_c...]
    pallas_call x0 -> x9, Pallas kernels: none -> 77.1 us  [the longest x5 30.6 us: local_call(): pl.pallas_call(kernel, name=name, out_shape=[jax.ShapeDtypeStruct(shape,...]
    psum x1 -> x0, blocking collectives: 32.6 us -> none  [on_device(): charge_total = lax.psum(jnp.sum(charges, axis=1), ('gx', 'gy'))]
    dynamic_update_slice x32 -> x0, local copies, waits for them, and re-layouts: 27.4 us -> none  [on_device(): block_re, block_im, sums_re, sums_im = lax.map(one_block, wave_blocks)]
    ppermute x8 -> x0, starting transfers between devices: 12.6 us -> none  [from_behind(): return lax.ppermute(value, axis, pairs)]
  transfers between devices with their start and end apart: 9 -> 0, of which waited for: 5 -> 0; matrix products, arithmetic and copies ran while one was open for 3% -> 0% of each run, Pallas kernels for 0% -> 0%
where the time goes in v1:
time: 83.3 us; the launch traced here: 82.9 us
  Pallas kernels  77.1 us (93%)
  local copies, waits for them, and re-layouts  4.02 us (5%)
  between operations  0.91 us (1%)
  other arithmetic  0.88 us (1%)
    pallas_call x5, Pallas kernels, local_call(): pl.pallas_call(kernel, name=name, out_shape=[jax.ShapeDtypeStruct(shape,...  30.6 us
    pallas_call x2, Pallas kernels, gather_blocks(): pl.pallas_call(functools.partial(gather_kernel, nx, ny), name=name, out_s...  29.7 us
    pallas_call x2, Pallas kernels, swap_blocks(): pl.pallas_call(functools.partial(swap_kernel, sign, nx, ny), name='ghosts...  16.7 us
    unnamed x31, local copies, waits for them, and re-layouts  3.44 us

profile of v1, /device:TPU:0, one launch (start us, length us, event | category | flops | bytes accessed | tf_op | source)
XLA Modules:
  0.0 82.9 jit_solution(6448948982866602733)
XLA Ops:
  0.6 0.0 copy-start.11
  0.6 0.0 copy-start.12
  0.7 0.0 copy-start.8
  0.7 0.0 copy-start
  0.7 0.0 copy-start.9
  0.7 0.0 copy-start.10
  0.7 0.0 copy-start.13
  0.7 0.0 copy-start.6
  0.7 0.0 copy-start.7
  0.7 0.0 copy-start.1
  0.7 0.8 convert_bitcast_fusion.1
  1.5 0.4 copy.28
  1.9 0.1 maximum_bitcast_fusion
  2.0 0.1 copy.25.anchor_ref
  2.2 0.1 pick_ghosts.1.in_ref
  2.2 0.0 copy-start.2
  2.3 0.6 copy-done.2
  2.9 9.5 %ghosts_out.1.ghost_ref = f32[8,8,128]{2,1,0:T(8,128)} custom-call(f32[8,8,128]{2,1,0:T(8,128)} %copy-done.2), custom_call_target="tpu_custom_call" | custom-call | tf_op jit(solution)/shard_map/ghosts_out/pallas_call | solution.py:141
  12.3 0.0 copy-done.10
  12.3 0.1 copy.26.pw_ref
  12.4 0.1 copy.27.ro_ref
  12.6 0.7 copy-done.4
  13.3 5.6 %short_range.1 = (f32[72,256]{1,0:T(8,128)S(1)}, f32[1,256]{1,0:T(1,128)S(1)}, f32[5,64,256]{2,1,0:T(8,128)S(1)}, f32[64,256]{1,0:T(8,128)S(1)}, f32[24,8,256]{2,1,0:T(8,128)S(1)}) custom-call(f32[4,256]{1,0:T(4,128)S(1)} %pad_maximum_fusion.record_ref, f32[8,8,128]{2,1,0:T(8,128)S(1)} %copy-done.4, s32[64,256]{1,0:T(8,128)S(1)} %bitcast.28, ...), custom_call_target="tpu_custom_call" | custom-call | tf_op jit(solution)/shard_map/short_range/pallas_call | solution.py:488
  19.0 15.2 %gather_charges.1 = f32[4,4,72,256]{3,2,1,0:T(8,128)S(1)} custom-call(f32[72,256]{1,0:T(8,128)S(1)} %get-tuple-element.12.in_ref.block_ref), custom_call_target="tpu_custom_call" | custom-call | tf_op jit(solution)/shard_map/gather_charges/pallas_call | solution.py:215
  34.2 7.8 %structure.1 = (f32[1,64,256]{2,1,0:T(8,128)S(1)}, f32[64,128]{1,0:T(8,128)S(1)}) custom-call(f32[16,72,256]{2,1,0:T(8,128)S(1)} %bitcast.25, f32[128,3]{1,0:T(8,128)S(1)} %dynamic-slice_bitcast_fusion.cols_ref, f32[1,8,128]{2,1,0:T(8,128)S(1)} %pad_dynamic-slice_fusion.rows_ref), custom_call_target="tpu_custom_call" | custom-call | tf_op jit(solution)/shard_map/structure/pallas_call | solution.py:488
  42.0 14.5 %gather_structure.1 = f32[4,4,64,256]{3,2,1,0:T(8,128)S(1)} custom-call(f32[64,256]{1,0:T(8,128)S(1)} %bitcast.30), custom_call_target="tpu_custom_call" | custom-call | tf_op jit(solution)/shard_map/gather_structure/pallas_call | solution.py:215
  56.5 16.8 %gradients.1 = (f32[1,256]{1,0:T(1,128)}, f32[8,256]{1,0:T(8,128)S(1)}, f32[8,8,128]{2,1,0:T(8,128)S(1)}) custom-call(f32[16,64,256]{2,1,0:T(8,128)S(1)} %bitcast.27, f32[2048,3]{1,0:T(8,128)S(1)} %bitcast.26, f32[16,8,128]{2,1,0:T(8,128)S(1)} %pad.4.rows_ref, f32[72,256]{1,0:T(8,128)S(1)} %get-tuple-element.12.in_ref.block_ref, ...), custom_call_target="tpu_custom_call" | custom-call | tf_op jit(solution)/shard_map/gradients/pallas_call | solution.py:488
  73.4 0.6 copy-done.5
  74.0 7.3 %ghosts_back.1.back_ref = f32[8,8,128]{2,1,0:T(8,128)} custom-call(f32[8,8,128]{2,1,0:T(8,128)} %copy-done.5), custom_call_target="tpu_custom_call" | custom-call | tf_op jit(solution)/shard_map/ghosts_back/pallas_call | solution.py:141
  81.3 0.7 copy-done.3
  82.0 0.2 owners.1
  82.3 0.6 copy.31
  (18 shorter events, 0.1 us)
Async XLA Ops:
  0.6 1.5 %copy-start.11 = (f32[3,1,1,256]{3,2,1,0:T(1,128)S(1)}, f32[3,1,1,256]{3,2,1,0:T(1,128)}, u32[]{:S(2)}) copy-start(f32[3,1,1,256]{3,2,1,0:T(1,128)} %param.11) | copy-start | bytes 9220
  0.6 1.5 %copy-start.12 = (s32[1,1,256]{2,1,0:T(1,128)S(1)}, s32[1,1,256]{2,1,0:T(1,128)}, u32[]{:S(2)}) copy-start(s32[1,1,256]{2,1,0:T(1,128)} %param.12) | copy-start | bytes 3076
  0.7 1.5 %copy-start.8 = (s32[1,1,8,128]{3,2,1,0:T(8,128)S(1)}, s32[1,1,8,128]{3,2,1,0:T(8,128)}, u32[]{:S(2)}) copy-start(s32[1,1,8,128]{3,2,1,0:T(8,128)} %param.15) | copy-start | bytes 12292
  0.7 11.9 %copy-start = (s32[1,1,64,256]{3,2,1,0:T(8,128)S(1)}, s32[1,1,64,256]{3,2,1,0:T(8,128)}, u32[]{:S(2)}) copy-start(s32[1,1,64,256]{3,2,1,0:T(8,128)} %param.13) | copy-start | bytes 196612
  0.7 11.9 %copy-start.9 = (s32[1,1,256]{2,1,0:T(1,128)S(1)}, s32[1,1,256]{2,1,0:T(1,128)}, u32[]{:S(2)}) copy-start(s32[1,1,256]{2,1,0:T(1,128)} %param.14) | copy-start | bytes 3076
  0.7 11.6 %copy-start.10 = (f32[128,64]{0,1:T(8,128)S(1)}, f32[128,64]{0,1:T(8,128)}, u32[]{:S(2)}) copy-start(f32[128,64]{0,1:T(8,128)} %param.19) | copy-start | bytes 98308
  0.7 11.7 %copy-start.13 = (f32[64]{0:T(128)S(1)}, f32[64]{0:T(128)}, u32[]{:S(2)}) copy-start(f32[64]{0:T(128)} %param.20) | copy-start | bytes 772
  0.7 11.8 %copy-start.6 = (f32[8,64]{1,0:T(8,128)S(1)}, f32[8,64]{1,0:T(8,128)}, u32[]{:S(2)}) copy-start(f32[8,64]{1,0:T(8,128)} %emb_ref.3) | copy-start | bytes 6148
  0.7 11.8 %copy-start.7 = (f32[8,64]{1,0:T(8,128)S(1)}, f32[8,64]{1,0:T(8,128)}, u32[]{:S(2)}) copy-start(f32[8,64]{1,0:T(8,128)} %rw_ref.3) | copy-start | bytes 6148
  0.7 11.8 %copy-start.1 = (f32[64,64]{1,0:T(8,128)S(1)}, f32[64,64]{1,0:T(8,128)}, u32[]{:S(2)}) copy-start(f32[64,64]{1,0:T(8,128)} %cw_ref.3) | copy-start | bytes 49156
  2.2 0.6 copy-start.2
  12.6 0.8 copy-start.4
  73.4 0.6 copy-start.5
  81.3 0.8 copy-start.3

commit v2 on v1

--- a/solution.py
+++ b/solution.py
@@ -147,88 +147,6 @@
         scratch_shapes=[pltpu.SemaphoreType.DMA((count,)), pltpu.SemaphoreType.DMA((count,))],
         compiler_params=pltpu.CompilerParams(collective_id=collective_id, has_side_effects=True),
     )(blocks)
-
-
-def gather_kernel(nx, ny, in_ref, out_ref, own_sem, line_sem, cross_sem, pair_sem, recv_sem):
-    gx, gy = lax.axis_index("gx"), lax.axis_index("gy")
-    chips = ny // 2
-    core = lax.rem(gy, 2)
-    chip = gy // 2
-    peer = chip * 2 + (1 - core)
-    order = sorted(range(1, nx), key=lambda step: min(step, nx - step))
-    lines = [lax.rem(gx + step, nx) for step in order]
-    crosses = [lax.rem(chip + step, chips) * 2 + core for step in range(1, chips)]
-    partners = [{"gx": x} for x in lines] + [{"gy": y} for y in crosses] + [{"gy": peer}]
-    barrier = pltpu.get_barrier_semaphore()
-    for partner in partners:
-        pl.semaphore_signal(barrier, inc=1, device_id=partner, device_id_type=MESH)
-    pl.semaphore_wait(barrier, len(partners))
-
-    def remote(source, slot_x, slot_y, send, device):
-        return pltpu.make_async_remote_copy(
-            src_ref=source,
-            dst_ref=out_ref.at[slot_x, slot_y],
-            send_sem=send,
-            recv_sem=recv_sem.at[slot_x, slot_y],
-            device_id=device,
-            device_id_type=MESH,
-        )
-
-    def arrived(slot_x, slot_y):
-        remote(
-            out_ref.at[slot_x, slot_y], slot_x, slot_y, recv_sem.at[slot_x, slot_y], {"gy": peer}
-        ).wait_recv()
-
-    sent = []
-
-    def send(source, slot_x, slot_y, semaphore, device):
-        copy = remote(source, slot_x, slot_y, semaphore, device)
-        copy.start()
-        sent.append(copy)
-
-    own = pltpu.make_async_copy(in_ref, out_ref.at[gx, gy], own_sem)
-    for index, x in enumerate(lines):
-        send(in_ref, gx, gy, line_sem.at[index], {"gx": x})
-    for index, y in enumerate(crosses):
-        send(in_ref, gx, gy, cross_sem.at[0, index], {"gy": y})
-    send(in_ref, gx, gy, pair_sem.at[0, 0], {"gy": peer})
-    own.start()
-    for row, x in enumerate(lines):
-        arrived(x, gy)
-        for index, y in enumerate(crosses):
-            send(out_ref.at[x, gy], x, gy, cross_sem.at[row + 1, index], {"gy": y})
-        send(out_ref.at[x, gy], x, gy, pair_sem.at[row + 1, 0], {"gy": peer})
-    for row, x in enumerate([gx] + lines):
-        for index, y in enumerate(crosses):
-            arrived(x, y)
-            send(out_ref.at[x, y], x, y, pair_sem.at[row, index + 1], {"gy": peer})
-    for x in [gx] + lines:
-        for step in range(chips):
-            arrived(x, lax.rem(chip + step, chips) * 2 + (1 - core))
-    own.wait()
-    for copy in sent:
-        copy.wait_send()
-
-
-def gather_blocks(block, nx, ny, collective_id, name):
-    chips = ny // 2
-    return pl.pallas_call(
-        functools.partial(gather_kernel, nx, ny),
-        name=name,
-        out_shape=jax.ShapeDtypeStruct((nx, ny) + block.shape, F32),
-        in_specs=[pl.BlockSpec(memory_space=VMEM)],
-        out_specs=pl.BlockSpec(memory_space=VMEM),
-        scratch_shapes=[
-            pltpu.SemaphoreType.DMA,
-            pltpu.SemaphoreType.DMA((nx - 1,)),
-            pltpu.SemaphoreType.DMA((nx, max(chips - 1, 1))),
-            pltpu.SemaphoreType.DMA((nx, chips)),
-            pltpu.SemaphoreType.DMA((nx, ny)),
-        ],
-        compiler_params=pltpu.CompilerParams(
-            collective_id=collective_id, has_side_effects=True, vmem_limit_bytes=VMEM_LIMIT
-        ),
-    )(block)
 
 
 def mixing_of(radial_weight, embedding):
@@ -312,32 +230,14 @@
         gp_ref[x * basis : (x + 1) * basis] = grad.reshape(basis, species, atoms)
 
 
-def structure_kernel(neutralise, total, channels, spans, blocks_ref, cols_ref, rows_ref, out_ref, mean_ref):
-    domains = blocks_ref.shape[0]
-    wave_blocks = out_ref.shape[0]
-    atoms = blocks_ref.shape[2]
-    if neutralise:
-        summed = blocks_ref[0, :channels, :]
-        for d in range(1, domains):
-            summed = summed + blocks_ref[d, :channels, :]
-        mean = jnp.sum(summed, axis=1, keepdims=True) / total
-    else:
-        mean = jnp.zeros((channels, 1), F32)
-    mean_ref[...] = jnp.broadcast_to(mean, mean_ref.shape)
-
+def structure_kernel(total, channels, spans, block_ref, cols_ref, rows_ref, out_ref):
     def one_block(w, carry):
         cols = cols_ref[pl.ds(pl.multiple_of(w * LANES, LANES), LANES), :]
-
-        def add_domain(d, running):
-            block = blocks_ref[d]
-            turns = cols[:, 0:1] * (block[channels : channels + 1] * (1.0 / spans[0]))
-            turns = turns + cols[:, 1:2] * (block[channels + 1 : channels + 2] * (1.0 / spans[1]))
-            turns = turns + cols[:, 2:3] * (block[channels + 2 : channels + 3] * (1.0 / spans[2]))
-            cosine, sine = cos_sin_turns(turns)
-            waves = jnp.concatenate([cosine, sine], axis=0)
-            return running + dot3(block[:channels] - mean, waves, ((1,), (1,)))
-
-        summed = lax.fori_loop(0, domains, add_domain, jnp.zeros((channels, 2 * LANES), F32))
+        turns = jnp.zeros((LANES, block_ref.shape[1]), F32)
+        for x in range(3):
+            placed = block_ref[channels + x : channels + x + 1, :]
+            turns = turns + cols[:, x : x + 1] * (placed * (1.0 / spans[x]))
+        waves = jnp.concatenate(cos_sin_turns(turns), axis=0)
         rows = rows_ref[w]
         squared = jnp.zeros((1, LANES), F32)
         for x in range(3):
@@ -345,10 +245,11 @@
             squared = squared + wave * wave
         weight = jnp.exp(-0.5 * SCREENING * SCREENING * squared) / (squared + 1.0)
         weight = weight * (1.0 / math.sqrt(total))
-        out_ref[w] = summed * jnp.concatenate([weight, weight], axis=1)
+        factors = dot3(block_ref[:channels, :], waves, ((1,), (1,)))
+        out_ref[w] = factors * jnp.concatenate([weight, weight], axis=1)
         return carry
 
-    lax.fori_loop(0, wave_blocks, one_block, 0)
+    lax.fori_loop(0, out_ref.shape[0], one_block, 0)
 
 
 def back_kernel(
@@ -472,16 +373,388 @@
             ghost_ref[d, x : x + 1, :] = summed[row : row + 1, :]
 
 
+def owned(values, rows, atoms):
+    ids = lax.broadcasted_iota(jnp.int32, (atoms, rows.shape[1]), 0)
+    onehot = jnp.where(ids == rows, 1.0, 0.0).astype(BF16)
+    halves = jnp.concatenate(split_bf16(values), axis=0)
+    part = lax.dot_general(halves, onehot, (((1,), (1,)), ((), ())), preferred_element_type=F32)
+    return part[:SUBLANES] + part[SUBLANES:]
+
+
 def owners_kernel(back_ref, rows_ref, own_ref, out_ref):
-    atoms = own_ref.shape[1]
     total = own_ref[...]
     for d in range(back_ref.shape[0]):
-        spots = lax.broadcasted_iota(jnp.int32, (atoms, rows_ref.shape[1]), 0)
-        onehot = jnp.where(spots == rows_ref[d : d + 1, :], 1.0, 0.0).astype(BF16)
-        values = jnp.concatenate(split_bf16(back_ref[d]), axis=0)
-        part = lax.dot_general(values, onehot, (((1,), (1,)), ((), ())), preferred_element_type=F32)
-        total = total + part[:SUBLANES] + part[SUBLANES:]
+        total = total + owned(back_ref[d], rows_ref[d : d + 1, :], own_ref.shape[1])
     out_ref[...] = -total[:3]
+
+
+class Spread:
+    def __init__(self, nx, ny, buffer, line_sem, cross_sem, pair_sem, recv_sem):
+        self.gx, self.gy = lax.axis_index("gx"), lax.axis_index("gy")
+        self.nx, self.chips = nx, ny // 2
+        self.core = lax.rem(self.gy, 2)
+        self.chip = self.gy // 2
+        self.peer = self.chip * 2 + (1 - self.core)
+        order = sorted(range(1, nx), key=lambda step: min(step, nx - step))
+        self.lines = [lax.rem(self.gx + step, nx) for step in order]
+        self.crosses = [
+            lax.rem(self.chip + step, self.chips) * 2 + self.core for step in range(1, self.chips)
+        ]
+        self.buffer = buffer
+        self.line_sem, self.cross_sem, self.pair_sem = line_sem, cross_sem, pair_sem
+        self.recv_sem = recv_sem
+        self.sent = []
+
+    def remote(self, x, y, send_sem, device):
+        return pltpu.make_async_remote_copy(
+            src_ref=self.buffer.at[x, y],
+            dst_ref=self.buffer.at[x, y],
+            send_sem=send_sem,
+            recv_sem=self.recv_sem.at[x, y],
+            device_id=device,
+            device_id_type=MESH,
+        )
+
+    def send(self, x, y, send_sem, device):
+        copy = self.remote(x, y, send_sem, device)
+        copy.start()
+        self.sent.append(copy)
+
+    def arrived(self, x, y):
+        self.remote(x, y, self.line_sem.at[0], {"gy": self.peer}).wait_recv()
+
+    def to_chip(self, x, row):
+        for index, y in enumerate(self.crosses):
+            self.send(x, self.gy, self.cross_sem.at[row, index], {"gy": y})
+        self.send(x, self.gy, self.pair_sem.at[row, 0], {"gy": self.peer})
+
+    def start(self):
+        for index, x in enumerate(self.lines):
+            self.send(self.gx, self.gy, self.line_sem.at[index], {"gx": x})
+        self.to_chip(self.gx, 0)
+
+    def take_lines(self, beside):
+        for row, x in enumerate(self.lines):
+            self.arrived(x, self.gy)
+            self.to_chip(x, row + 1)
+            beside(row, x, self.gy)
+
+    def take_crosses(self, beside):
+        for row, x in enumerate([self.gx] + self.lines):
+            for index, y in enumerate(self.crosses):
+                self.arrived(x, y)
+                self.send(x, y, self.pair_sem.at[row, index + 1], {"gy": self.peer})
+                beside(row, x, y)
+
+    def take_pairs(self, beside, carry):
+        def one(j, running):
+            x = lax.rem(self.gx + j // self.chips, self.nx)
+            y = lax.rem(self.chip + j % self.chips, self.chips) * 2 + (1 - self.core)
+            self.arrived(x, y)
+            return beside(x, y, running)
+
+        return lax.fori_loop(0, self.nx * self.chips, one, carry)
+
+    def finish(self):
+        for copy in self.sent:
+            copy.wait_send()
+
+
+def fused_kernel(
+    nx, ny, spans, total, block_ref, cols_ref, rows_ref, short_ref, geo_ref, codes_ref,
+    counts_ref, gd_ref, gp_ref, rw_ref, emb_ref, cw_ref, owner_ref,
+    energy_ref, force_ref,
+    charge_ref, struct_ref, waves_ref, slices_ref, pair_ref, onehot_ref, gd_rows_ref,
+    acc_ref, ghost_ref, back_ref,
+    line1, cross1, pair1, recv1, line2, cross2, pair2, recv2, swap_send, swap_recv,
+):
+    slots, atoms = codes_ref.shape
+    species, channels = emb_ref.shape
+    basis = rw_ref.shape[0]
+    wave_blocks = rows_ref.shape[0]
+    gx, gy = lax.axis_index("gx"), lax.axis_index("gy")
+    mine = gx * ny + gy
+
+    def other(sx, sy):
+        return {"gx": lax.rem(gx + sx + nx, nx), "gy": lax.rem(gy + sy + ny, ny)}
+
+    barrier = pltpu.get_barrier_semaphore()
+    steps = {(sx, 0) for sx in range(1, nx)} | {(0, sy) for sy in range(1, ny)}
+    steps |= {(sx % nx, sy % ny) for sx, sy in DIRECTIONS}
+    for sx, sy in sorted(steps):
+        pl.semaphore_signal(barrier, inc=1, device_id=other(sx, sy), device_id_type=MESH)
+    charge_ref[gx, gy] = block_ref[...]
+    pl.semaphore_wait(barrier, len(steps))
+    first = Spread(nx, ny, charge_ref, line1, cross1, pair1, recv1)
+    second = Spread(nx, ny, struct_ref, line2, cross2, pair2, recv2)
+    first.start()
+
+    def table(cols, placed):
+        turns = cols[:, 0:1] * (placed[0:1] * (1.0 / spans[0]))
+        turns = turns + cols[:, 1:2] * (placed[1:2] * (1.0 / spans[1]))
+        turns = turns + cols[:, 2:3] * (placed[2:3] * (1.0 / spans[2]))
+        cosine, sine = cos_sin_turns(turns)
+        return split_bf16(jnp.concatenate([cosine, sine], axis=0))
+
+    own_placed = block_ref[channels:, :]
+
+    def own_waves(w, carry):
+        cols = cols_ref[pl.ds(pl.multiple_of(w * LANES, LANES), LANES), :]
+        high, low = table(cols, own_placed)
+        waves_ref[w, 0] = high
+        waves_ref[w, 1] = low
+        return carry
+
+    def slice_waves(x, y):
+        cols = cols_ref[pl.ds(pl.multiple_of(mine * LANES, LANES), LANES), :]
+        high, low = table(cols, charge_ref[x, y, channels:, :])
+        slices_ref[x, y, 0] = high
+        slices_ref[x, y, 1] = low
+
+    slice_waves(gx, gy)
+    early = wave_blocks * 3 // 8
+    lax.fori_loop(0, early, own_waves, 0)
+    first.take_lines(lambda row, x, y: slice_waves(x, y))
+    first.take_crosses(lambda row, x, y: slice_waves(x, y))
+
+    def take_charge(x, y, carry):
+        slice_waves(x, y)
+        return carry
+
+    first.take_pairs(take_charge, 0)
+
+    summed = lax.fori_loop(
+        0,
+        wave_blocks,
+        lambda d, running: running + charge_ref[d // ny, d % ny, :channels, :],
+        jnp.zeros((channels, atoms), F32),
+    )
+    mean = jnp.sum(summed, axis=1, keepdims=True) / total
+
+    def split_dot(a_high, a_low, b_high, b_low, dims):
+        dot = functools.partial(
+            lax.dot_general, dimension_numbers=(dims, ((), ())), preferred_element_type=F32
+        )
+        return dot(a_high, b_high) + (dot(a_high, b_low) + dot(a_low, b_high))
+
+    def add_domain(d, running):
+        x, y = d // ny, d % ny
+        high, low = split_bf16(charge_ref[x, y, :channels, :] - mean)
+        return running + split_dot(
+            high, low, slices_ref[x, y, 0], slices_ref[x, y, 1], ((1,), (1,))
+        )
+
+    factors = lax.fori_loop(
+        0, wave_blocks, add_domain, jnp.zeros((channels, 2 * LANES), F32), unroll=2
+    )
+    rows = rows_ref[mine]
+    squared = jnp.zeros((1, LANES), F32)
+    for x in range(3):
+        wave = rows[x : x + 1] * (2.0 * math.pi / spans[x])
+        squared = squared + wave * wave
+    weight = jnp.exp(-0.5 * SCREENING * SCREENING * squared) / (squared + 1.0)
+    weight = weight * (1.0 / math.sqrt(total))
+    struct_ref[gx, gy] = factors * jnp.concatenate([weight, weight], axis=1)
+    second.start()
+
+    def near_rows(i):
+        start = pl.multiple_of(i * SUBLANES, SUBLANES)
+        window = pl.ds(start, SUBLANES)
+        unit = [geo_ref[x, window, :] for x in range(3)]
+        radius = geo_ref[3, window, :]
+        kind = geo_ref[4, window, :]
+        masks = [kind == float(s) for s in range(1, species)]
+        slot = lax.broadcasted_iota(jnp.int32, (SUBLANES, atoms), 0) + start
+        live = jnp.where(slot < counts_ref[...], 1.0, 0.0)
+
+        def of_kind(rows):
+            chosen = jnp.broadcast_to(rows[0:1, :], (SUBLANES, atoms))
+            for s in range(1, species):
+                chosen = jnp.where(masks[s - 1], rows[s : s + 1, :], chosen)
+            return chosen
+
+        def radial_of(b):
+            offset = radius - BASIS_STEP * b
+            radial = jnp.exp(-BASIS_WIDTH * (offset * offset)) * live
+            return radial, (-2.0 * BASIS_WIDTH) * offset * radial
+
+        return window, unit, radius, of_kind, radial_of
+
+    gd_rows_ref[...] = gd_ref[...].reshape(basis, species, atoms)
+
+    def short_pairs(i, carry):
+        window, unit, radius, of_kind, radial_of = near_rows(i)
+        along = jnp.zeros((SUBLANES, atoms), F32)
+        turn = [jnp.zeros((SUBLANES, atoms), F32) for x in range(3)]
+        for b in range(basis):
+            radial, slope = radial_of(b)
+            whole = of_kind(gd_rows_ref[b])
+            for x in range(3):
+                polar = of_kind(gp_ref[x * basis + b])
+                whole = whole + unit[x] * polar
+                turn[x] = turn[x] + radial * polar
+            along = along + slope * whole
+        inverse = 1.0 / radius
+        swing = turn[0] * unit[0] + turn[1] * unit[1] + turn[2] * unit[2]
+        radial_part = along - swing * inverse
+        for x in range(3):
+            pair_ref[x, window, :] = unit[x] * radial_part + turn[x] * inverse
+        return carry
+
+    def spots(n, carry):
+        low = codes_ref[pl.ds(n, 1), :] % LANES
+        ids = lax.broadcasted_iota(jnp.int32, (LANES, atoms), 0)
+        onehot_ref[n] = jnp.where(ids == low, 1.0, 0.0).astype(BF16)
+        return carry
+
+    cuts = [early + (wave_blocks - early) * k // nx for k in range(nx + 1)]
+    lax.fori_loop(cuts[0], cuts[1], own_waves, 0)
+    second.take_lines(
+        lambda row, x, y: lax.fori_loop(cuts[row + 1], cuts[row + 2], own_waves, 0)
+    )
+    groups = slots // SUBLANES
+    shares = [groups * k // nx for k in range(nx + 1)]
+    second.take_crosses(
+        lambda row, x, y: lax.fori_loop(shares[row], shares[row + 1], short_pairs, 0)
+    )
+    lax.fori_loop(0, slots, spots, 0, unroll=2)
+
+    neutral = block_ref[:channels, :] - mean
+    neutral_high, neutral_low = split_bf16(neutral)
+
+    def add_waves(x, y, carry):
+        potential, pulled = carry
+        w = x * ny + y
+        high, low = waves_ref[w, 0], waves_ref[w, 1]
+        s_high, s_low = split_bf16(struct_ref[x, y])
+        potential = potential + split_dot(s_high, s_low, high, low, ((1,), (0,)))
+        projected = split_dot(s_high, s_low, neutral_high, neutral_low, ((0,), (0,)))
+        waves = high.astype(F32) + low.astype(F32)
+        torque = waves[:LANES] * projected[LANES:] - waves[LANES:] * projected[:LANES]
+        return potential, pulled + dot3(rows_ref[w], torque, ((1,), (0,)))
+
+    chips = ny // 2
+    core, chip = lax.rem(gy, 2), gy // 2
+
+    def same_core(j, carry):
+        return add_waves(
+            lax.rem(gx + j // chips, nx), lax.rem(chip + j % chips, chips) * 2 + core, carry
+        )
+
+    carry = (jnp.zeros((channels, atoms), F32), jnp.zeros((SUBLANES, atoms), F32))
+    carry = lax.fori_loop(0, nx * chips, same_core, carry)
+    potential, pulled = second.take_pairs(add_waves, carry)
+
+    energy_ref[...] = short_ref[...] + 0.5 * jnp.sum(neutral * potential, axis=0, keepdims=True)
+    mixing = mixing_of(rw_ref[...], emb_ref[...])
+    norm = 1.0 / math.sqrt(slots)
+    density_grad = norm * dot_nn(mixing, dot_nn(cw_ref[...], potential))
+    gd_rows_ref[...] = density_grad.reshape(basis, species, atoms)
+    chunks = acc_ref.shape[0] // 6
+    acc_ref[...] = jnp.zeros(acc_ref.shape, F32)
+    chunk_ids = lax.broadcasted_iota(jnp.int32, (chunks, atoms), 0)
+
+    def scatter_rows(i, centres):
+        window, unit, radius, of_kind, radial_of = near_rows(i)
+        along = jnp.zeros((SUBLANES, atoms), F32)
+        for b in range(basis):
+            along = along + radial_of(b)[1] * of_kind(gd_rows_ref[b])
+        grads = [pair_ref[x, window, :] + unit[x] * along for x in range(3)]
+        added = None
+        high_codes = codes_ref[window, :] // LANES
+        for k in range(SUBLANES):
+            here = chunk_ids == high_codes[k : k + 1, :]
+            values = jnp.concatenate(
+                [jnp.where(here, grads[x][k : k + 1, :], 0.0) for x in range(3)], axis=0
+            )
+            part = lax.dot_general(
+                jnp.concatenate(split_bf16(values), axis=0),
+                onehot_ref[i * SUBLANES + k],
+                (((1,), (1,)), ((), ())),
+                preferred_element_type=F32,
+            )
+            added = part if added is None else added + part
+        acc_ref[...] += added
+        return tuple(centre + grad for centre, grad in zip(centres, grads))
+
+    centres = lax.fori_loop(
+        0, groups, scatter_rows, tuple(jnp.zeros((SUBLANES, atoms), F32) for x in range(3))
+    )
+    acc = acc_ref[: 3 * chunks, :] + acc_ref[3 * chunks :, :]
+    own_chunks = atoms // LANES
+    for d in range(len(DIRECTIONS)):
+        picked = [acc[x * chunks + own_chunks + d : x * chunks + own_chunks + d + 1] for x in range(3)]
+        filler = jnp.zeros((SUBLANES - 3, ghost_ref.shape[2]), F32)
+        ghost_ref[d] = jnp.concatenate(picked + [filler], axis=0)
+    swaps = [
+        pltpu.make_async_remote_copy(
+            src_ref=ghost_ref.at[d],
+            dst_ref=back_ref.at[d],
+            send_sem=swap_send.at[d],
+            recv_sem=swap_recv.at[d],
+            device_id=other(-sx, -sy),
+            device_id_type=MESH,
+        )
+        for d, (sx, sy) in enumerate(DIRECTIONS)
+    ]
+    for swap in swaps:
+        swap.start()
+    rows = []
+    for x in range(3):
+        received = jnp.concatenate(
+            [acc[x * chunks + h : x * chunks + h + 1, :] for h in range(own_chunks)], axis=1
+        )
+        centre = jnp.sum(centres[x], axis=0, keepdims=True)
+        rows.append(received - centre + pulled[x : x + 1, :] * (2.0 * math.pi / spans[x]))
+    sums = jnp.concatenate(rows + [jnp.zeros((SUBLANES - 3, atoms), F32)], axis=0)
+    first.finish()
+    second.finish()
+    for d, swap in enumerate(swaps):
+        swap.wait()
+        sums = sums + owned(back_ref[d], owner_ref[d : d + 1, :], atoms)
+    force_ref[...] = -sums[:3]
+
+
+def spread_semaphores(nx, ny):
+    chips = ny // 2
+    return [
+        pltpu.SemaphoreType.DMA((nx - 1,)),
+        pltpu.SemaphoreType.DMA((nx, max(chips - 1, 1))),
+        pltpu.SemaphoreType.DMA((nx, chips)),
+        pltpu.SemaphoreType.DMA((nx, ny)),
+    ]
+
+
+def fused_call(nx, ny, spans, total, chunks, outs, *args):
+    block, cols, rows, short, geo, codes, counts, gd, gp, rw, emb, cw, owner = args
+    slots, atoms = codes.shape
+    species, channels = emb.shape
+    directions, width = owner.shape
+    scratch = [
+        pltpu.VMEM((nx, ny) + block.shape, F32),
+        pltpu.VMEM((nx, ny, channels, 2 * LANES), F32),
+        pltpu.VMEM((rows.shape[0], 2, 2 * LANES, atoms), BF16),
+        pltpu.VMEM((nx, ny, 2, 2 * LANES, atoms), BF16),
+        pltpu.VMEM((3, slots, atoms), F32),
+        pltpu.VMEM((slots, LANES, atoms), BF16),
+        pltpu.VMEM((rw.shape[0], species, atoms), F32),
+        pltpu.VMEM((6 * chunks, LANES), F32),
+        pltpu.VMEM((directions, SUBLANES, width), F32),
+        pltpu.VMEM((directions, SUBLANES, width), F32),
+    ]
+    scratch += spread_semaphores(nx, ny) + spread_semaphores(nx, ny)
+    scratch += [pltpu.SemaphoreType.DMA((directions,)), pltpu.SemaphoreType.DMA((directions,))]
+    return pl.pallas_call(
+        functools.partial(fused_kernel, nx, ny, spans, total),
+        name="charges_to_forces",
+        out_shape=[jax.ShapeDtypeStruct(shape, F32) for shape in outs],
+        in_specs=[pl.BlockSpec(memory_space=VMEM)] * len(args),
+        out_specs=[pl.BlockSpec(memory_space=VMEM)] * len(outs),
+        scratch_shapes=scratch,
+        compiler_params=pltpu.CompilerParams(
+            collective_id=1, has_side_effects=True, vmem_limit_bytes=VMEM_LIMIT
+        ),
+    )(*args)
 
 
 def local_call(kernel, name, outs, scratch, *args):
@@ -553,35 +826,27 @@
         embedding, radial_weight, product_weight, readout, charge_weight,
     )
     wave_blocks = waves // LANES
+    chunks = 16 * -(-(atoms // LANES + directions * width // LANES) // 16)
     if wave_blocks == domains:
-        mine = gx * ny + gy
-        blocks = gather_blocks(block, nx, ny, 1, "gather_charges")
-        struct, mean = local_call(
-            functools.partial(structure_kernel, True, total_atoms, channels, spans),
-            "structure",
-            [(1, channels, 2 * LANES), (channels, LANES)],
-            [],
-            blocks.reshape(domains, channels + SUBLANES, atoms),
-            lax.dynamic_slice_in_dim(wave_cols, mine * LANES, LANES, axis=0),
-            lax.dynamic_slice_in_dim(wave_rows, mine, 1, axis=0),
-        )
-        struct = gather_blocks(struct[0], nx, ny, 2, "gather_structure")
-        struct = struct.reshape(wave_blocks, channels, 2 * LANES)
-    else:
-        charge_total = lax.psum(jnp.sum(block[:channels], axis=1, keepdims=True), ("gx", "gy"))
-        mean = jnp.broadcast_to(charge_total / total_atoms, (channels, LANES))
-        neutral = jnp.concatenate([block[:channels] - mean[:, :1], block[channels:]], axis=0)
-        struct, unused = local_call(
-            functools.partial(structure_kernel, False, total_atoms, channels, spans),
-            "structure",
-            [(wave_blocks, channels, 2 * LANES), (channels, LANES)],
-            [],
-            neutral[None],
-            wave_cols,
-            wave_rows,
-        )
-        struct = lax.psum(struct, ("gx", "gy"))
-    chunks = 16 * -(-(atoms // LANES + directions * width // LANES) // 16)
+        energy, forces = fused_call(
+            nx, ny, spans, total_atoms, chunks, [(1, atoms), (3, atoms)],
+            block, wave_cols, wave_rows, short_energy, geometry, codes, used,
+            density_grad, polar_grad, radial_weight, embedding, charge_weight, ghost_rows,
+        )
+        return (forces[:, None, None, :], energy[None])
+    charge_total = lax.psum(jnp.sum(block[:channels], axis=1, keepdims=True), ("gx", "gy"))
+    mean = jnp.broadcast_to(charge_total / total_atoms, (channels, LANES))
+    neutral = jnp.concatenate([block[:channels] - mean[:, :1], block[channels:]], axis=0)
+    (struct,) = local_call(
+        functools.partial(structure_kernel, total_atoms, channels, spans),
+        "structure",
+        [(wave_blocks, channels, 2 * LANES)],
+        [],
+        neutral,
+        wave_cols,
+        wave_rows,
+    )
+    struct = lax.psum(struct, ("gx", "gy"))
     energy, own_grad, ghost_grad = local_call(
         functools.partial(back_kernel, spans),
         "gradients",

time: 83.3 us -> 72.8 us (0.87)
  Pallas kernels: 77.1 us -> 65.6 us
  local copies, waits for them, and re-layouts: 4.02 us -> 5.91 us
    pallas_call x5 -> x2, Pallas kernels: 30.6 us -> 5.7 us  [local_call(): pl.pallas_call(kernel, name=name, out_shape=[jax.ShapeDtypeStruct(shape,...]
    pallas_call x2 -> x1, Pallas kernels: 29.7 us -> 50.4 us  [fused_call(): pl.pallas_call(functools.partial(fused_kernel, nx, ny, spans, total), nam...]
    pallas_call x2 -> x1, Pallas kernels: 16.7 us -> 9.47 us  [swap_blocks(): pl.pallas_call(functools.partial(swap_kernel, sign, nx, ny), name='ghosts...]
    unnamed x31 -> x30, local copies, waits for them, and re-layouts: 3.44 us -> 5.35 us
where the time goes in v2:
time: 72.8 us; the launch traced here: 72.3 us
  Pallas kernels  65.6 us (90%)
  local copies, waits for them, and re-layouts  5.91 us (8%)
  between operations  0.74 us (1%)
    pallas_call x1, Pallas kernels, fused_call(): pl.pallas_call(functools.partial(fused_kernel, nx, ny, spans, total), nam...  50.4 us
    pallas_call x1, Pallas kernels, swap_blocks(): pl.pallas_call(functools.partial(swap_kernel, sign, nx, ny), name='ghosts...  9.47 us
    pallas_call x2, Pallas kernels, local_call(): pl.pallas_call(kernel, name=name, out_shape=[jax.ShapeDtypeStruct(shape,...  5.7 us
    unnamed x30, local copies, waits for them, and re-layouts  5.35 us

profile of v2, /device:TPU:0, one launch (start us, length us, event | category | flops | bytes accessed | tf_op | source)
XLA Modules:
  0.0 72.3 jit_solution(2516638433468620879)
XLA Ops:
  0.6 0.1 maximum_bitcast_fusion
  0.7 0.0 copy-start.11
  0.7 0.0 copy-start.10
  0.7 0.7 copy-done.11
  1.4 0.1 copy.25.anchor_ref
  1.5 0.0 copy-done.10
  1.5 0.0 copy-start.6
  1.5 0.7 copy-done.6
  2.2 0.1 pick_ghosts.1.in_ref
  2.3 0.0 copy-start.2
  2.3 0.6 copy-done.2
  2.9 9.5 %ghosts_out.1.ghost_ref = f32[8,8,128]{2,1,0:T(8,128)} custom-call(f32[8,8,128]{2,1,0:T(8,128)} %copy-done.2), custom_call_target="tpu_custom_call" | custom-call | tf_op jit(solution)/shard_map/ghosts_out/pallas_call | solution.py:141
  12.3 0.0 copy-done.12
  12.4 0.0 copy-start.8
  12.4 0.1 copy.27.ro_ref
  12.5 0.7 copy-done.8
  13.1 0.1 copy.26.pw_ref
  13.2 0.7 copy-done.9
  13.9 0.0 copy-start
  13.9 0.0 copy-start.1
  13.9 0.0 copy-start.4
  14.0 0.7 copy-done.3
  14.6 0.0 copy-done.5
  14.6 0.0 copy-done.7
  14.6 0.1 copy-done
  14.8 0.0 copy-done.1
  14.8 0.0 copy-done.4
  14.8 5.6 %short_range.1 = (f32[72,256]{1,0:T(8,128)S(1)}, f32[1,256]{1,0:T(1,128)S(1)}, f32[5,64,256]{2,1,0:T(8,128)S(1)}, f32[64,256]{1,0:T(8,128)S(1)}, f32[24,8,256]{2,1,0:T(8,128)S(1)}) custom-call(f32[4,256]{1,0:T(4,128)S(1)} %pad_maximum_fusion.record_ref, f32[8,8,128]{2,1,0:T(8,128)S(1)} %copy-done.3, s32[64,256]{1,0:T(8,128)S(1)} %bitcast.21, ...), custom_call_target="tpu_custom_call" | custom-call | tf_op jit(solution)/shard_map/short_range/pallas_call | solution.py:761
  20.4 0.4 copy.28
  20.8 50.4 %charges_to_forces.1 = (f32[1,256]{1,0:T(1,128)S(1)}, f32[3,256]{1,0:T(4,128)S(1)}) custom-call(f32[72,256]{1,0:T(8,128)S(1)} %get-tuple-element.9.block_ref, f32[2048,3]{1,0:T(8,128)S(1)} %bitcast.20, f32[16,8,128]{2,1,0:T(8,128)S(1)} %pad.4.rows_ref, f32[1,256]{1,0:T(1,128)S(1)} %get-tuple-element.10.short_ref, ...), custom_call_target="tpu_custom_call" | custom-call | tf_op jit(solution)/shard_map/charges_to_forces/pallas_call | solution.py:747
  71.2 0.6 copy.30
  71.8 0.6 copy.35
  (10 shorter events, 0.0 us)
Async XLA Ops:
  0.7 0.7 copy-start.11
  0.7 0.8 %copy-start.10 = (f32[3,1,1,256]{3,2,1,0:T(1,128)S(1)}, f32[3,1,1,256]{3,2,1,0:T(1,128)}, u32[]{:S(2)}) copy-start(f32[3,1,1,256]{3,2,1,0:T(1,128)} %param.11) | copy-start | bytes 9220
  1.5 0.7 copy-start.6
  2.3 0.6 copy-start.2
  2.9 9.5 %copy-start.12 = (f32[64]{0:T(128)S(1)}, f32[64]{0:T(128)}, u32[]{:S(2)}) copy-start(f32[64]{0:T(128)} %param.20) | copy-start | bytes 772
  12.4 0.8 %copy-start.8 = (f32[128,64]{0,1:T(8,128)S(1)}, f32[128,64]{0,1:T(8,128)}, u32[]{:S(2)}) copy-start(f32[128,64]{0,1:T(8,128)} %param.19) | copy-start | bytes 98308
  13.1 0.8 %copy-start.9 = (s32[3,2048]{1,0:T(4,128)S(1)}, s32[3,2048]{1,0:T(4,128)}, u32[]{:S(2)}) copy-start(s32[3,2048]{1,0:T(4,128)} %param.16) | copy-start | bytes 73732
  13.9 0.8 %copy-start.3 = (f32[8,8,128]{2,1,0:T(8,128)S(1)}, f32[8,8,128]{2,1,0:T(8,128)}, u32[]{:S(2)}) copy-start(f32[8,8,128]{2,1,0:T(8,128)} %ghosts_out.1.ghost_ref) | copy-start | bytes 98308
  13.9 0.8 %copy-start.5 = (f32[8,64]{1,0:T(8,128)S(1)}, f32[8,64]{1,0:T(8,128)}, u32[]{:S(2)}) copy-start(f32[8,64]{1,0:T(8,128)} %rw_ref.3) | copy-start | bytes 6148
  13.9 0.8 %copy-start.7 = (s32[1,1,256]{2,1,0:T(1,128)S(1)}, s32[1,1,256]{2,1,0:T(1,128)}, u32[]{:S(2)}) copy-start(s32[1,1,256]{2,1,0:T(1,128)} %param.14) | copy-start | bytes 3076
  13.9 0.9 %copy-start = (s32[1,1,64,256]{3,2,1,0:T(8,128)S(1)}, s32[1,1,64,256]{3,2,1,0:T(8,128)}, u32[]{:S(2)}) copy-start(s32[1,1,64,256]{3,2,1,0:T(8,128)} %param.13) | copy-start | bytes 196612
  13.9 0.9 %copy-start.1 = (f32[64,64]{1,0:T(8,128)S(1)}, f32[64,64]{1,0:T(8,128)}, u32[]{:S(2)}) copy-start(f32[64,64]{1,0:T(8,128)} %cw_ref.3) | copy-start | bytes 49156
  13.9 0.9 %copy-start.4 = (f32[8,64]{1,0:T(8,128)S(1)}, f32[8,64]{1,0:T(8,128)}, u32[]{:S(2)}) copy-start(f32[8,64]{1,0:T(8,128)} %emb_ref.3) | copy-start | bytes 6148

commit v3 on v2

--- a/solution.py
+++ b/solution.py
@@ -464,7 +464,7 @@
     nx, ny, spans, total, block_ref, cols_ref, rows_ref, short_ref, geo_ref, codes_ref,
     counts_ref, gd_ref, gp_ref, rw_ref, emb_ref, cw_ref, owner_ref,
     energy_ref, force_ref,
-    charge_ref, struct_ref, waves_ref, slices_ref, pair_ref, onehot_ref, gd_rows_ref,
+    charge_ref, struct_ref, waves_ref, wide_ref, slim_ref, sum_ref, long_ref, pair_ref, onehot_ref, gd_rows_ref,
     acc_ref, ghost_ref, back_ref,
     line1, cross1, pair1, recv1, line2, cross2, pair2, recv2, swap_send, swap_recv,
 ):
@@ -505,11 +505,24 @@
         waves_ref[w, 1] = low
         return carry
 
+    shift = jnp.sum(block_ref[:channels, :], axis=1, keepdims=True) * (1.0 / atoms)
+    ones = jnp.ones((channels, atoms), BF16)
+    blank = jnp.zeros((channels, atoms), BF16)
+    wide_ref[...] = jnp.zeros(wide_ref.shape, F32)
+    slim_ref[...] = jnp.zeros(slim_ref.shape, F32)
+    sum_ref[...] = jnp.zeros(sum_ref.shape, F32)
+
+    def over_atoms(a, b):
+        return lax.dot_general(a, b, (((1,), (1,)), ((), ())), preferred_element_type=F32)
+
     def slice_waves(x, y):
         cols = cols_ref[pl.ds(pl.multiple_of(mine * LANES, LANES), LANES), :]
         high, low = table(cols, charge_ref[x, y, channels:, :])
-        slices_ref[x, y, 0] = high
-        slices_ref[x, y, 1] = low
+        charges = charge_ref[x, y, :channels, :]
+        sum_ref[...] += charges
+        q_high, q_low = split_bf16(charges - shift)
+        wide_ref[...] += over_atoms(high, jnp.concatenate([q_high, ones, q_low, blank], axis=0))
+        slim_ref[...] += over_atoms(low, jnp.concatenate([q_high, ones], axis=0))
 
     slice_waves(gx, gy)
     early = wave_blocks * 3 // 8
@@ -523,30 +536,12 @@
 
     first.take_pairs(take_charge, 0)
 
-    summed = lax.fori_loop(
-        0,
-        wave_blocks,
-        lambda d, running: running + charge_ref[d // ny, d % ny, :channels, :],
-        jnp.zeros((channels, atoms), F32),
-    )
-    mean = jnp.sum(summed, axis=1, keepdims=True) / total
-
-    def split_dot(a_high, a_low, b_high, b_low, dims):
-        dot = functools.partial(
-            lax.dot_general, dimension_numbers=(dims, ((), ())), preferred_element_type=F32
-        )
-        return dot(a_high, b_high) + (dot(a_high, b_low) + dot(a_low, b_high))
-
-    def add_domain(d, running):
-        x, y = d // ny, d % ny
-        high, low = split_bf16(charge_ref[x, y, :channels, :] - mean)
-        return running + split_dot(
-            high, low, slices_ref[x, y, 0], slices_ref[x, y, 1], ((1,), (1,))
-        )
-
-    factors = lax.fori_loop(
-        0, wave_blocks, add_domain, jnp.zeros((channels, 2 * LANES), F32), unroll=2
-    )
+    mean = jnp.sum(sum_ref[...], axis=1, keepdims=True) / total
+    wide = wide_ref[...]
+    main = jnp.transpose(wide[:, : 2 * channels] + slim_ref[...])
+    rest = jnp.transpose(wide[:, 2 * channels :])
+    factors = main[:channels] + rest[:channels]
+    factors = factors + (shift - mean) * main[channels : channels + 1]
     rows = rows_ref[mine]
     squared = jnp.zeros((1, LANES), F32)
     for x in range(3):
@@ -620,18 +615,23 @@
     lax.fori_loop(0, slots, spots, 0, unroll=2)
 
     neutral = block_ref[:channels, :] - mean
-    neutral_high, neutral_low = split_bf16(neutral)
+    long_ref[...] = jnp.zeros(long_ref.shape, F32)
 
     def add_waves(x, y, carry):
-        potential, pulled = carry
         w = x * ny + y
-        high, low = waves_ref[w, 0], waves_ref[w, 1]
-        s_high, s_low = split_bf16(struct_ref[x, y])
-        potential = potential + split_dot(s_high, s_low, high, low, ((1,), (0,)))
-        projected = split_dot(s_high, s_low, neutral_high, neutral_low, ((0,), (0,)))
-        waves = high.astype(F32) + low.astype(F32)
-        torque = waves[:LANES] * projected[LANES:] - waves[LANES:] * projected[:LANES]
-        return potential, pulled + dot3(rows_ref[w], torque, ((1,), (0,)))
+        struct = struct_ref[x, y]
+        turned = jnp.concatenate([struct[:, LANES:], -struct[:, :LANES]], axis=1)
+        rows = rows_ref[w]
+        rows = jnp.concatenate([rows, rows], axis=1)
+        parts = [struct] + [turned * rows[axis : axis + 1] for axis in range(3)]
+        high, low = split_bf16(jnp.concatenate(parts, axis=0))
+        both = jnp.dot(
+            jnp.concatenate([high, low], axis=0), waves_ref[w, 0], preferred_element_type=F32
+        )
+        fine = jnp.dot(high, waves_ref[w, 1], preferred_element_type=F32)
+        count = high.shape[0]
+        long_ref[...] += both[:count] + both[count:] + fine
+        return carry
 
     chips = ny // 2
     core, chip = lax.rem(gy, 2), gy // 2
@@ -641,9 +641,13 @@
             lax.rem(gx + j // chips, nx), lax.rem(chip + j % chips, chips) * 2 + core, carry
         )
 
-    carry = (jnp.zeros((channels, atoms), F32), jnp.zeros((SUBLANES, atoms), F32))
-    carry = lax.fori_loop(0, nx * chips, same_core, carry)
-    potential, pulled = second.take_pairs(add_waves, carry)
+    lax.fori_loop(0, nx * chips, same_core, 0)
+    second.take_pairs(add_waves, 0)
+    potential = long_ref[:channels, :]
+    pulled = [
+        jnp.sum(neutral * long_ref[(x + 1) * channels : (x + 2) * channels, :], axis=0, keepdims=True)
+        for x in range(3)
+    ]
 
     energy_ref[...] = short_ref[...] + 0.5 * jnp.sum(neutral * potential, axis=0, keepdims=True)
     mixing = mixing_of(rw_ref[...], emb_ref[...])
@@ -705,7 +709,7 @@
             [acc[x * chunks + h : x * chunks + h + 1, :] for h in range(own_chunks)], axis=1
         )
         centre = jnp.sum(centres[x], axis=0, keepdims=True)
-        rows.append(received - centre + pulled[x : x + 1, :] * (2.0 * math.pi / spans[x]))
+        rows.append(received - centre + pulled[x] * (2.0 * math.pi / spans[x]))
     sums = jnp.concatenate(rows + [jnp.zeros((SUBLANES - 3, atoms), F32)], axis=0)
     first.finish()
     second.finish()
@@ -734,7 +738,10 @@
         pltpu.VMEM((nx, ny) + block.shape, F32),
         pltpu.VMEM((nx, ny, channels, 2 * LANES), F32),
         pltpu.VMEM((rows.shape[0], 2, 2 * LANES, atoms), BF16),
-        pltpu.VMEM((nx, ny, 2, 2 * LANES, atoms), BF16),
+        pltpu.VMEM((2 * LANES, 4 * channels), F32),
+        pltpu.VMEM((2 * LANES, 2 * channels), F32),
+        pltpu.VMEM((channels, atoms), F32),
+        pltpu.VMEM((4 * channels, atoms), F32),
         pltpu.VMEM((3, slots, atoms), F32),
         pltpu.VMEM((slots, LANES, atoms), BF16),
         pltpu.VMEM((rw.shape[0], species, atoms), F32),

time: 72.8 us -> 66.3 us (0.911)
  Pallas kernels: 65.6 us -> 59.2 us
    pallas_call x1, Pallas kernels: 50.4 us -> 44 us  [fused_call(): pl.pallas_call(functools.partial(fused_kernel, nx, ny, spans, total), nam...]
where the time goes in v3:
time: 66.3 us; the launch traced here: 65.9 us
  Pallas kernels  59.2 us (89%)
  local copies, waits for them, and re-layouts  5.91 us (9%)
  between operations  0.74 us (1%)
    pallas_call x1, Pallas kernels, fused_call(): pl.pallas_call(functools.partial(fused_kernel, nx, ny, spans, total), nam...  44 us
    pallas_call x1, Pallas kernels, swap_blocks(): pl.pallas_call(functools.partial(swap_kernel, sign, nx, ny), name='ghosts...  9.47 us
    pallas_call x2, Pallas kernels, local_call(): pl.pallas_call(kernel, name=name, out_shape=[jax.ShapeDtypeStruct(shape,...  5.7 us
    unnamed x30, local copies, waits for them, and re-layouts  5.35 us

profile of v3, /device:TPU:0, one launch (start us, length us, event | category | flops | bytes accessed | tf_op | source)
XLA Modules:
  0.0 65.9 jit_solution(7946762708504830053)
XLA Ops:
  0.6 0.1 maximum_bitcast_fusion
  0.7 0.0 copy-start.11
  0.7 0.0 copy-start.10
  0.7 0.7 %copy-done.11 = s32[1,1,256]{2,1,0:T(1,128)S(1)} copy-done((s32[1,1,256]{2,1,0:T(1,128)S(1)}, s32[1,1,256]{2,1,0:T(1,128)}, u32[]{:S(2)}) %copy-start.11) | copy-done | bytes 1048
  1.4 0.1 copy.25.anchor_ref
  1.5 0.0 copy-done.10
  1.5 0.0 copy-start.6
  1.5 0.7 %copy-done.6 = s32[1,1,8,128]{3,2,1,0:T(8,128)S(1)} copy-done((s32[1,1,8,128]{3,2,1,0:T(8,128)S(1)}, s32[1,1,8,128]{3,2,1,0:T(8,128)}, u32[]{:S(2)}) %copy-start.6) | copy-done | bytes 4120
  2.2 0.1 pick_ghosts.1.in_ref
  2.3 0.0 copy-start.2
  2.3 0.6 copy-done.2
  2.9 9.5 %ghosts_out.1.ghost_ref = f32[8,8,128]{2,1,0:T(8,128)} custom-call(f32[8,8,128]{2,1,0:T(8,128)} %copy-done.2), custom_call_target="tpu_custom_call" | custom-call | tf_op jit(solution)/shard_map/ghosts_out/pallas_call | solution.py:141
  12.3 0.0 copy-done.12
  12.4 0.0 copy-start.8
  12.4 0.1 copy.27.ro_ref
  12.5 0.7 copy-done.8
  13.1 0.1 copy.26.pw_ref
  13.2 0.7 %copy-done.9 = s32[3,2048]{1,0:T(4,128)S(1)} copy-done((s32[3,2048]{1,0:T(4,128)S(1)}, s32[3,2048]{1,0:T(4,128)}, u32[]{:S(2)}) %copy-start.9) | copy-done | bytes 24600
  13.9 0.0 copy-start
  13.9 0.0 copy-start.1
  13.9 0.0 copy-start.4
  14.0 0.7 %copy-done.3 = f32[8,8,128]{2,1,0:T(8,128)S(1)} copy-done((f32[8,8,128]{2,1,0:T(8,128)S(1)}, f32[8,8,128]{2,1,0:T(8,128)}, u32[]{:S(2)}) %copy-start.3) | copy-done | bytes 32792
  14.6 0.0 copy-done.5
  14.6 0.0 copy-done.7
  14.6 0.1 copy-done
  14.8 0.0 copy-done.1
  14.8 0.0 copy-done.4
  14.8 5.6 %short_range.1 = (f32[72,256]{1,0:T(8,128)S(1)}, f32[1,256]{1,0:T(1,128)S(1)}, f32[5,64,256]{2,1,0:T(8,128)S(1)}, f32[64,256]{1,0:T(8,128)S(1)}, f32[24,8,256]{2,1,0:T(8,128)S(1)}) custom-call(f32[4,256]{1,0:T(4,128)S(1)} %pad_maximum_fusion.record_ref, f32[8,8,128]{2,1,0:T(8,128)S(1)} %copy-done.3, s32[64,256]{1,0:T(8,128)S(1)} %bitcast.21, ...), custom_call_target="tpu_custom_call" | custom-call | tf_op jit(solution)/shard_map/short_range/pallas_call | solution.py:768
  20.4 0.4 copy.28
  20.8 44.0 %charges_to_forces.1 = (f32[1,256]{1,0:T(1,128)S(1)}, f32[3,256]{1,0:T(4,128)S(1)}) custom-call(f32[72,256]{1,0:T(8,128)S(1)} %get-tuple-element.9.block_ref, f32[2048,3]{1,0:T(8,128)S(1)} %bitcast.20, f32[16,8,128]{2,1,0:T(8,128)S(1)} %pad.4.rows_ref, f32[1,256]{1,0:T(1,128)S(1)} %get-tuple-element.10.short_ref, ...), custom_call_target="tpu_custom_call" | custom-call | tf_op jit(solution)/shard_map/charges_to_forces/pallas_call | solution.py:754
  64.8 0.6 copy.30
  65.3 0.6 copy.35
  (10 shorter events, 0.0 us)
Async XLA Ops:
  0.7 0.7 %copy-start.11 = (s32[1,1,256]{2,1,0:T(1,128)S(1)}, s32[1,1,256]{2,1,0:T(1,128)}, u32[]{:S(2)}) copy-start(s32[1,1,256]{2,1,0:T(1,128)} %param.12) | copy-start | bytes 3076
  0.7 0.8 %copy-start.10 = (f32[3,1,1,256]{3,2,1,0:T(1,128)S(1)}, f32[3,1,1,256]{3,2,1,0:T(1,128)}, u32[]{:S(2)}) copy-start(f32[3,1,1,256]{3,2,1,0:T(1,128)} %param.11) | copy-start | bytes 9220
  1.5 0.7 %copy-start.6 = (s32[1,1,8,128]{3,2,1,0:T(8,128)S(1)}, s32[1,1,8,128]{3,2,1,0:T(8,128)}, u32[]{:S(2)}) copy-start(s32[1,1,8,128]{3,2,1,0:T(8,128)} %param.15) | copy-start | bytes 12292
  2.3 0.6 copy-start.2
  2.9 9.5 %copy-start.12 = (f32[64]{0:T(128)S(1)}, f32[64]{0:T(128)}, u32[]{:S(2)}) copy-start(f32[64]{0:T(128)} %param.20) | copy-start | bytes 772
  12.4 0.8 %copy-start.8 = (f32[128,64]{0,1:T(8,128)S(1)}, f32[128,64]{0,1:T(8,128)}, u32[]{:S(2)}) copy-start(f32[128,64]{0,1:T(8,128)} %param.19) | copy-start | bytes 98308
  13.1 0.8 %copy-start.9 = (s32[3,2048]{1,0:T(4,128)S(1)}, s32[3,2048]{1,0:T(4,128)}, u32[]{:S(2)}) copy-start(s32[3,2048]{1,0:T(4,128)} %param.16) | copy-start | bytes 73732
  13.9 0.8 %copy-start.3 = (f32[8,8,128]{2,1,0:T(8,128)S(1)}, f32[8,8,128]{2,1,0:T(8,128)}, u32[]{:S(2)}) copy-start(f32[8,8,128]{2,1,0:T(8,128)} %ghosts_out.1.ghost_ref) | copy-start | bytes 98308
  13.9 0.8 %copy-start.5 = (f32[8,64]{1,0:T(8,128)S(1)}, f32[8,64]{1,0:T(8,128)}, u32[]{:S(2)}) copy-start(f32[8,64]{1,0:T(8,128)} %rw_ref.3) | copy-start | bytes 6148
  13.9 0.8 %copy-start.7 = (s32[1,1,256]{2,1,0:T(1,128)S(1)}, s32[1,1,256]{2,1,0:T(1,128)}, u32[]{:S(2)}) copy-start(s32[1,1,256]{2,1,0:T(1,128)} %param.14) | copy-start | bytes 3076
  13.9 0.9 %copy-start = (s32[1,1,64,256]{3,2,1,0:T(8,128)S(1)}, s32[1,1,64,256]{3,2,1,0:T(8,128)}, u32[]{:S(2)}) copy-start(s32[1,1,64,256]{3,2,1,0:T(8,128)} %param.13) | copy-start | bytes 196612
  13.9 0.9 %copy-start.1 = (f32[64,64]{1,0:T(8,128)S(1)}, f32[64,64]{1,0:T(8,128)}, u32[]{:S(2)}) copy-start(f32[64,64]{1,0:T(8,128)} %cw_ref.3) | copy-start | bytes 49156
  13.9 0.9 %copy-start.4 = (f32[8,64]{1,0:T(8,128)S(1)}, f32[8,64]{1,0:T(8,128)}, u32[]{:S(2)}) copy-start(f32[8,64]{1,0:T(8,128)} %emb_ref.3) | copy-start | bytes 6148

commit v4 on v3

--- a/solution.py
+++ b/solution.py
@@ -446,14 +446,18 @@
                 self.send(x, y, self.pair_sem.at[row, index + 1], {"gy": self.peer})
                 beside(row, x, y)
 
-    def take_pairs(self, beside, carry):
-        def one(j, running):
-            x = lax.rem(self.gx + j // self.chips, self.nx)
-            y = lax.rem(self.chip + j % self.chips, self.chips) * 2 + (1 - self.core)
+    def take_pairs(self, beside, first, last):
+        count = last - first
+
+        def one(j, carry):
+            x = lax.rem(self.gx + j // count, self.nx)
+            y = lax.rem(self.chip + first + j % count, self.chips) * 2 + (1 - self.core)
             self.arrived(x, y)
-            return beside(x, y, running)
-
-        return lax.fori_loop(0, self.nx * self.chips, one, carry)
+            beside(x, y)
+            return carry
+
+        if count > 0:
+            lax.fori_loop(0, self.nx * count, one, 0)
 
     def finish(self):
         for copy in self.sent:
@@ -528,13 +532,14 @@
     early = wave_blocks * 3 // 8
     lax.fori_loop(0, early, own_waves, 0)
     first.take_lines(lambda row, x, y: slice_waves(x, y))
-    first.take_crosses(lambda row, x, y: slice_waves(x, y))
-
-    def take_charge(x, y, carry):
+
+    def charge_cross(row, x, y):
         slice_waves(x, y)
-        return carry
-
-    first.take_pairs(take_charge, 0)
+        if row == nx - 2:
+            first.take_pairs(slice_waves, 0, 1)
+
+    first.take_crosses(charge_cross)
+    first.take_pairs(slice_waves, 1, ny // 2)
 
     mean = jnp.sum(sum_ref[...], axis=1, keepdims=True) / total
     wide = wide_ref[...]
@@ -608,16 +613,10 @@
         lambda row, x, y: lax.fori_loop(cuts[row + 1], cuts[row + 2], own_waves, 0)
     )
     groups = slots // SUBLANES
-    shares = [groups * k // nx for k in range(nx + 1)]
-    second.take_crosses(
-        lambda row, x, y: lax.fori_loop(shares[row], shares[row + 1], short_pairs, 0)
-    )
-    lax.fori_loop(0, slots, spots, 0, unroll=2)
-
     neutral = block_ref[:channels, :] - mean
     long_ref[...] = jnp.zeros(long_ref.shape, F32)
 
-    def add_waves(x, y, carry):
+    def add_waves(x, y):
         w = x * ny + y
         struct = struct_ref[x, y]
         turned = jnp.concatenate([struct[:, LANES:], -struct[:, :LANES]], axis=1)
@@ -631,18 +630,36 @@
         fine = jnp.dot(high, waves_ref[w, 1], preferred_element_type=F32)
         count = high.shape[0]
         long_ref[...] += both[:count] + both[count:] + fine
-        return carry
 
     chips = ny // 2
     core, chip = lax.rem(gy, 2), gy // 2
 
-    def same_core(j, carry):
-        return add_waves(
-            lax.rem(gx + j // chips, nx), lax.rem(chip + j % chips, chips) * 2 + core, carry
-        )
-
-    lax.fori_loop(0, nx * chips, same_core, 0)
-    second.take_pairs(add_waves, 0)
+    def same_core(first_chip, last_chip):
+        count = last_chip - first_chip
+
+        def one(j, carry):
+            x = lax.rem(gx + j // count, nx)
+            add_waves(x, lax.rem(chip + first_chip + j % count, chips) * 2 + core)
+            return carry
+
+        if count > 0:
+            lax.fori_loop(0, nx * count, one, 0)
+
+    tasks = [
+        lambda: lax.fori_loop(0, groups, short_pairs, 0),
+        lambda: (lax.fori_loop(0, slots, spots, 0, unroll=2), same_core(0, 1)),
+        lambda: second.take_pairs(add_waves, 0, 1),
+    ]
+
+    def struct_cross(row, x, y):
+        if tasks:
+            tasks.pop(0)()
+
+    second.take_crosses(struct_cross)
+    for task in tasks:
+        task()
+    same_core(1, chips)
+    second.take_pairs(add_waves, 1, chips)
     potential = long_ref[:channels, :]
     pulled = [
         jnp.sum(neutral * long_ref[(x + 1) * channels : (x + 2) * channels, :], axis=0, keepdims=True)

time: 66.3 us -> 64 us (0.965)
  Pallas kernels: 59.2 us -> 56.8 us
    pallas_call x1, Pallas kernels: 44 us -> 41.6 us  [fused_call(): pl.pallas_call(functools.partial(fused_kernel, nx, ny, spans, total), nam...]
where the time goes in v4:
time: 64 us; the launch traced here: 63.6 us
  Pallas kernels  56.8 us (89%)
  local copies, waits for them, and re-layouts  5.91 us (9%)
  between operations  0.74 us (1%)
    pallas_call x1, Pallas kernels, fused_call(): pl.pallas_call(functools.partial(fused_kernel, nx, ny, spans, total), nam...  41.6 us
    pallas_call x1, Pallas kernels, swap_blocks(): pl.pallas_call(functools.partial(swap_kernel, sign, nx, ny), name='ghosts...  9.47 us
    pallas_call x2, Pallas kernels, local_call(): pl.pallas_call(kernel, name=name, out_shape=[jax.ShapeDtypeStruct(shape,...  5.7 us
    unnamed x30, local copies, waits for them, and re-layouts  5.35 us

profile of v4, /device:TPU:0, one launch (start us, length us, event | category | flops | bytes accessed | tf_op | source)
XLA Modules:
  0.0 63.6 jit_solution(5056316295650847590)
XLA Ops:
  0.6 0.1 maximum_bitcast_fusion
  0.7 0.0 copy-start.11
  0.7 0.0 copy-start.10
  0.7 0.7 %copy-done.11 = s32[1,1,256]{2,1,0:T(1,128)S(1)} copy-done((s32[1,1,256]{2,1,0:T(1,128)S(1)}, s32[1,1,256]{2,1,0:T(1,128)}, u32[]{:S(2)}) %copy-start.11) | copy-done | bytes 1048
  1.4 0.1 copy.25.anchor_ref
  1.5 0.0 copy-done.10
  1.5 0.0 copy-start.6
  1.5 0.7 %copy-done.6 = s32[1,1,8,128]{3,2,1,0:T(8,128)S(1)} copy-done((s32[1,1,8,128]{3,2,1,0:T(8,128)S(1)}, s32[1,1,8,128]{3,2,1,0:T(8,128)}, u32[]{:S(2)}) %copy-start.6) | copy-done | bytes 4120
  2.2 0.1 pick_ghosts.1.in_ref
  2.3 0.0 copy-start.2
  2.3 0.6 copy-done.2
  2.9 9.5 %ghosts_out.1.ghost_ref = f32[8,8,128]{2,1,0:T(8,128)} custom-call(f32[8,8,128]{2,1,0:T(8,128)} %copy-done.2), custom_call_target="tpu_custom_call" | custom-call | tf_op jit(solution)/shard_map/ghosts_out/pallas_call | solution.py:141
  12.3 0.0 copy-done.12
  12.4 0.0 copy-start.8
  12.4 0.1 copy.27.ro_ref
  12.5 0.7 %copy-done.8 = f32[128,64]{0,1:T(8,128)S(1)} copy-done((f32[128,64]{0,1:T(8,128)S(1)}, f32[128,64]{0,1:T(8,128)}, u32[]{:S(2)}) %copy-start.8) | copy-done | bytes 32792
  13.1 0.1 copy.26.pw_ref
  13.2 0.7 %copy-done.9 = s32[3,2048]{1,0:T(4,128)S(1)} copy-done((s32[3,2048]{1,0:T(4,128)S(1)}, s32[3,2048]{1,0:T(4,128)}, u32[]{:S(2)}) %copy-start.9) | copy-done | bytes 24600
  13.9 0.0 copy-start
  13.9 0.0 copy-start.1
  13.9 0.0 copy-start.4
  14.0 0.7 %copy-done.3 = f32[8,8,128]{2,1,0:T(8,128)S(1)} copy-done((f32[8,8,128]{2,1,0:T(8,128)S(1)}, f32[8,8,128]{2,1,0:T(8,128)}, u32[]{:S(2)}) %copy-start.3) | copy-done | bytes 32792
  14.6 0.0 copy-done.5
  14.6 0.0 copy-done.7
  14.6 0.1 copy-done
  14.8 0.0 copy-done.1
  14.8 0.0 copy-done.4
  14.8 5.6 %short_range.1 = (f32[72,256]{1,0:T(8,128)S(1)}, f32[1,256]{1,0:T(1,128)S(1)}, f32[5,64,256]{2,1,0:T(8,128)S(1)}, f32[64,256]{1,0:T(8,128)S(1)}, f32[24,8,256]{2,1,0:T(8,128)S(1)}) custom-call(f32[4,256]{1,0:T(4,128)S(1)} %pad_maximum_fusion.record_ref, f32[8,8,128]{2,1,0:T(8,128)S(1)} %copy-done.3, s32[64,256]{1,0:T(8,128)S(1)} %bitcast.21, ...), custom_call_target="tpu_custom_call" | custom-call | tf_op jit(solution)/shard_map/short_range/pallas_call | solution.py:785
  20.4 0.4 copy.28
  20.8 41.6 %charges_to_forces.1 = (f32[1,256]{1,0:T(1,128)S(1)}, f32[3,256]{1,0:T(4,128)S(1)}) custom-call(f32[72,256]{1,0:T(8,128)S(1)} %get-tuple-element.9.block_ref, f32[2048,3]{1,0:T(8,128)S(1)} %bitcast.20, f32[16,8,128]{2,1,0:T(8,128)S(1)} %pad.4.rows_ref, f32[1,256]{1,0:T(1,128)S(1)} %get-tuple-element.10.short_ref, ...), custom_call_target="tpu_custom_call" | custom-call | tf_op jit(solution)/shard_map/charges_to_forces/pallas_call | solution.py:771
  62.4 0.6 copy.30
  63.0 0.6 copy.35
  (10 shorter events, 0.0 us)
Async XLA Ops:
  0.7 0.7 %copy-start.11 = (s32[1,1,256]{2,1,0:T(1,128)S(1)}, s32[1,1,256]{2,1,0:T(1,128)}, u32[]{:S(2)}) copy-start(s32[1,1,256]{2,1,0:T(1,128)} %param.12) | copy-start | bytes 3076
  0.7 0.8 %copy-start.10 = (f32[3,1,1,256]{3,2,1,0:T(1,128)S(1)}, f32[3,1,1,256]{3,2,1,0:T(1,128)}, u32[]{:S(2)}) copy-start(f32[3,1,1,256]{3,2,1,0:T(1,128)} %param.11) | copy-start | bytes 9220
  1.5 0.7 %copy-start.6 = (s32[1,1,8,128]{3,2,1,0:T(8,128)S(1)}, s32[1,1,8,128]{3,2,1,0:T(8,128)}, u32[]{:S(2)}) copy-start(s32[1,1,8,128]{3,2,1,0:T(8,128)} %param.15) | copy-start | bytes 12292
  2.3 0.6 copy-start.2
  2.9 9.5 %copy-start.12 = (f32[64]{0:T(128)S(1)}, f32[64]{0:T(128)}, u32[]{:S(2)}) copy-start(f32[64]{0:T(128)} %param.20) | copy-start | bytes 772
  12.4 0.8 %copy-start.8 = (f32[128,64]{0,1:T(8,128)S(1)}, f32[128,64]{0,1:T(8,128)}, u32[]{:S(2)}) copy-start(f32[128,64]{0,1:T(8,128)} %param.19) | copy-start | bytes 98308
  13.1 0.8 %copy-start.9 = (s32[3,2048]{1,0:T(4,128)S(1)}, s32[3,2048]{1,0:T(4,128)}, u32[]{:S(2)}) copy-start(s32[3,2048]{1,0:T(4,128)} %param.16) | copy-start | bytes 73732
  13.9 0.8 %copy-start.3 = (f32[8,8,128]{2,1,0:T(8,128)S(1)}, f32[8,8,128]{2,1,0:T(8,128)}, u32[]{:S(2)}) copy-start(f32[8,8,128]{2,1,0:T(8,128)} %ghosts_out.1.ghost_ref) | copy-start | bytes 98308
  13.9 0.8 %copy-start.5 = (f32[8,64]{1,0:T(8,128)S(1)}, f32[8,64]{1,0:T(8,128)}, u32[]{:S(2)}) copy-start(f32[8,64]{1,0:T(8,128)} %rw_ref.3) | copy-start | bytes 6148
  13.9 0.8 %copy-start.7 = (s32[1,1,256]{2,1,0:T(1,128)S(1)}, s32[1,1,256]{2,1,0:T(1,128)}, u32[]{:S(2)}) copy-start(s32[1,1,256]{2,1,0:T(1,128)} %param.14) | copy-start | bytes 3076
  13.9 0.9 %copy-start = (s32[1,1,64,256]{3,2,1,0:T(8,128)S(1)}, s32[1,1,64,256]{3,2,1,0:T(8,128)}, u32[]{:S(2)}) copy-start(s32[1,1,64,256]{3,2,1,0:T(8,128)} %param.13) | copy-start | bytes 196612
  13.9 0.9 %copy-start.1 = (f32[64,64]{1,0:T(8,128)S(1)}, f32[64,64]{1,0:T(8,128)}, u32[]{:S(2)}) copy-start(f32[64,64]{1,0:T(8,128)} %cw_ref.3) | copy-start | bytes 49156
  13.9 0.9 %copy-start.4 = (f32[8,64]{1,0:T(8,128)S(1)}, f32[8,64]{1,0:T(8,128)}, u32[]{:S(2)}) copy-start(f32[8,64]{1,0:T(8,128)} %emb_ref.3) | copy-start | bytes 6148
